TPU v7x, 128 devices: a whole 4x4x4 slice. The times are simulated.
128 devices in a mesh: table: 16 (over y, x), ctx: 8 (over z, core).
Axes of the slice: x: 4, y: 4, z: 4, core: 2. Of those that a mesh axis runs over, the one named last changes fastest.
Arguments:
- base_embed: bfloat16 [16, 1024, 2048], P('table', 'ctx'), may hold values from -6 to 6
- ngram_ids: int32 [16, 1024], P('table', 'ctx'), may hold values from 0 to 65535, as said below
- ngram_table: bfloat16 [65536, 2048], P(('table', 'ctx')), may hold values from -6 to 6
- embed_cot: bfloat16 [16, 1024, 2048], P('table', 'ctx'), may hold values from -6 to 6
- norm_gain: bfloat16 [2048], replicated, may hold values from 0.099609375 to 1.8984375
- w_qkv: bfloat16 [2048, 3072], replicated
Outputs:
- context: bfloat16 [16, 1024, 1024], P('table', 'ctx')
- table_grad: float32 [65536, 2048], P(('table', 'ctx'))
Inputs may be any that keep to these rules, and one draw needn't show every extreme that they name: `ngram_ids`: device o of the joined table and ctx axes holds rows o * 512 to (o + 1) * 512 - 1. In each device's block of 128 tokens at most 4 tokens name rows of one owner, and exactly 4 name rows of some owner.
All inputs are finite; a program needn't handle non-finite values.
Results may differ from a plain program's by a relative error of at most 0.0085.
The roundings to bfloat16 on the way count: a program that leaves them out, or rounds other values in their place, can miss the bound.
Values may be sent and summed in bfloat16 or wider, within the bound.
No kernel may reach another device: no remote copies, remote signals or barrier semaphores. Data moves between devices by JAX's collectives and lax.ppermute only.
A program may use at most 128 MiB of HBM per device.

v0:
```python
import jax
import jax.numpy as jnp
from jax import lax
from jax.sharding import PartitionSpec as P

HEAD = 128
HEADS = 8


def fetch_rows(asked, ngram_table):
    rows = ngram_table[jnp.clip(asked, 0, ngram_table.shape[0] - 1)]
    return lax.all_to_all(rows, ("table", "ctx"), split_axis=0, concat_axis=0, tiled=True)


def add_grads(asked, cot_rows, ngram_table):
    held = ngram_table.shape[0]
    flat_ids = asked.reshape(-1)
    target = jnp.where(flat_ids >= 0, flat_ids, held)
    grads = jnp.zeros((held, ngram_table.shape[1]), jnp.float32)
    return grads.at[target].add(
        cot_rows.reshape(flat_ids.shape[0], -1).astype(jnp.float32), mode="drop"
    )


def shards(base_embed, ngram_ids, ngram_table, embed_cot, norm_gain, w_qkv):
    tokens = ngram_ids.shape[1]
    width = base_embed.shape[2]
    held = ngram_table.shape[0]
    owners = lax.axis_size("table") * lax.axis_size("ctx")
    capacity = tokens // 32
    ids = ngram_ids[0]
    owner = ids // held
    onehot = (owner[:, None] == jnp.arange(owners, dtype=jnp.int32)[None, :]).astype(jnp.int32)
    before = jnp.sum((jnp.cumsum(onehot, axis=0) - onehot) * onehot, axis=1)
    slot = owner * capacity + before
    requests = (
        jnp.full((owners * capacity,), -1, jnp.int32)
        .at[slot]
        .set(ids % held)
        .reshape(owners, capacity)
    )
    cot_slots = (
        jnp.zeros((owners * capacity, width), jnp.bfloat16)
        .at[slot]
        .set(embed_cot[0])
        .reshape(owners, capacity, width)
    )
    asked = lax.all_to_all(requests, ("table", "ctx"), split_axis=0, concat_axis=0, tiled=True)
    got = fetch_rows(asked, ngram_table)
    cot_all = lax.all_to_all(cot_slots, ("table", "ctx"), split_axis=0, concat_axis=0, tiled=True)
    table_grad = add_grads(asked, cot_all, ngram_table)
    fetched = got.reshape(owners * capacity, width)[slot]
    summed = base_embed[0].astype(jnp.float32) + fetched.astype(jnp.float32)
    scale = lax.rsqrt(jnp.mean(summed * summed, axis=-1, keepdims=True) + 1e-05)
    normed = (summed * scale * norm_gain.astype(jnp.float32)).astype(jnp.bfloat16)
    projected = jnp.dot(normed, w_qkv, preferred_element_type=jnp.float32).astype(jnp.bfloat16)
    feats = HEADS * HEAD
    query = projected[:, :feats].reshape(tokens, HEADS, HEAD)
    keys = projected[:, feats : 2 * feats]
    values = projected[:, 2 * feats :]
    q_pos = lax.axis_index("ctx") * tokens + jnp.arange(tokens, dtype=jnp.int32)
    key_piece = lax.all_gather(keys, "ctx", axis=0, tiled=True)
    value_piece = lax.all_gather(values, "ctx", axis=0, tiled=True)
    count = key_piece.shape[0]
    key_heads = key_piece.reshape(count, HEADS, HEAD)
    value_heads = value_piece.reshape(count, HEADS, HEAD)
    top_old = jnp.full((HEADS, tokens), -1e30, jnp.float32)
    scores = jnp.einsum(
        "qhd,khd->hqk", query, key_heads, preferred_element_type=jnp.float32
    ) * HEAD ** (-0.5)
    k_pos = jnp.arange(count, dtype=jnp.int32)
    allowed = (k_pos[None, :] <= q_pos[:, None])[None, :, :]
    top_new = jnp.maximum(top_old, jnp.max(jnp.where(allowed, scores, -1e30), axis=2))
    weights = jnp.where(allowed, jnp.exp(scores - top_new[:, :, None]), 0.0)
    total_new = jnp.sum(weights, axis=2)
    mixed = jnp.einsum(
        "hqk,khd->hqd",
        weights.astype(jnp.bfloat16),
        value_heads,
        preferred_element_type=jnp.float32,
    )
    context = (
        (mixed / total_new[:, :, None])
        .transpose(1, 0, 2)
        .reshape(tokens, feats)
        .astype(jnp.bfloat16)
    )
    return (context[None], table_grad)


def solution(mesh):
    return jax.shard_map(
        shards,
        mesh=mesh,
        in_specs=(
            P("table", "ctx", None),
            P("table", "ctx"),
            P(("table", "ctx"), None),
            P("table", "ctx", None),
            P(),
            P(),
        ),
        out_specs=(P("table", "ctx", None), P(("table", "ctx"), None)),
        check_vma=False,
    )
```

profile of v0, /device:TPU:1, one launch (start us, length us, event | category | flops | bytes accessed | tf_op | source)
XLA Modules:
  0.0 177.7 jit_solution(10299505795123550455)
XLA Ops:
  9.1 1.0 scatter_custom_fusion
  10.2 20.7 %all_to_all.19 = s32[128,1,4]{2,1,0:T(1,128)S(1)} all-to-all(s32[128,1,4]{2,1,0:T(1,128)S(1)} %bitcast.76), channel_id=1, replica_groups=mesh['table'=16,'ctx'=8] {'table','ctx'}, dimensions={0} | all-to-all | bytes 4096 | tf_op jit(solution)/shard_map/all_to_all | solution.py:48
  31.4 0.9 fusion.36
  32.5 3.3 %gather_fusion = bf16[512,2048]{1,0:T(8,128)(2,1)} fusion(bf16[512,2048]{1,0:T(8,128)(2,1)S(1)} %copy-done, s32[1024]{0:T(1024)S(1)} %pad_clamp_fusion.1), kind=kCustom, calls=%fused_computation | custom fusion | bytes 4196352 | tf_op jit(solution)/shard_map/gather | solution.py:11
  35.7 4.1 %reshape.237 = bf16[128,4,2048]{2,1,0:T(4,128)(2,1)} reshape(bf16[512,2048]{1,0:T(8,128)(2,1)} %gather_fusion) | data formatting | bytes 4194304 | tf_op jit(solution)/shard_map/gather | solution.py:11
  39.9 5.7 %all-to-all-start.1 = ((bf16[128,4,2048]{2,1,0:T(4,128)(2,1)}), bf16[128,4,2048]{2,1,0:T(4,128)(2,1)}, u32[]{:S(2)}, u32[]{:S(2)}) async-start(bf16[128,4,2048]{2,1,0:T(4,128)(2,1)} %reshape.237), calls=%async_computation.1 | async-start | bytes 4194304 | tf_op jit(solution)/shard_map/all_to_all | solution.py:12
  45.6 29.9 %all-to-all-done.1 = bf16[128,4,2048]{2,1,0:T(4,128)(2,1)} async-done(((bf16[128,4,2048]{2,1,0:T(4,128)(2,1)}), bf16[128,4,2048]{2,1,0:T(4,128)(2,1)}, u32[]{:S(2)}, u32[]{:S(2)}) %all-to-all-start.1) | async-done | bytes 2097184 | tf_op jit(solution)/shard_map/all_to_all | solution.py:12
  75.6 3.9 %reshape.228 = bf16[512,2048]{1,0:T(8,128)(2,1)} reshape(bf16[128,4,2048]{2,1,0:T(4,128)(2,1)} %all-to-all-done.1) | data formatting | bytes 4194304 | tf_op jit(solution)/shard_map/reshape | solution.py:52
  79.5 3.3 %gather_fusion.1 = bf16[128,2048]{1,0:T(8,128)(2,1)S(1)} fusion(bf16[512,2048]{1,0:T(8,128)(2,1)} %reshape.228, s32[1024]{0:T(1024)S(1)} %pad_clamp_fusion), kind=kCustom, calls=%fused_computation.1 | custom fusion | bytes 1049088 | tf_op jit(solution)/shard_map/gather | solution.py:52
  83.1 6.5 %convolution_convert_fusion = bf16[128,3072]{1,0:T(8,128)(2,1)S(1)} fusion(bf16[2048,3072]{1,0:T(8,128)(2,1)} %param.11, bf16[128,2048]{1,0:T(8,128)(2,1)S(1)} %gather_fusion.1, bf16[1,128,2048]{2,1,0:T(8,128)(2,1)S(1)} %copy-done.2, f32[2048]{0:T(1024)S(1)} %convert_element_type.47, f32[128]{0:T(128)S(1)} %add_rsqrt_fusion), kind=kOutput, calls=%fused_computation.7 | convolution fusion | flops 1612578816 | bytes 14426624 | tf_op jit(solution)/shard_map/dot_general | solution.py:56
  89.6 0.9 slice_bitcast_fusion
  91.2 3.5 %scatter_custom_fusion.1 = bf16[512,2048]{1,0:T(8,128)(2,1)} fusion(s32[128]{0:T(128)S(1)} %fusion.33, bf16[]{:T(256)} %constant.65.clone.1, bf16[1,128,2048]{2,1,0:T(8,128)(2,1)} %param.9), kind=kCustom, calls=%fused_computation.22 | custom fusion | bytes 2621442 | tf_op jit(solution)/shard_map/scatter | solution.py:45
  94.8 4.1 %reshape.233 = bf16[128,4,2048]{2,1,0:T(4,128)(2,1)} reshape(bf16[512,2048]{1,0:T(8,128)(2,1)} %scatter_custom_fusion.1) | data formatting | bytes 4194304 | tf_op jit(solution)/shard_map/reshape | solution.py:46
  98.9 5.8 %all-to-all-start.2 = ((bf16[128,4,2048]{2,1,0:T(4,128)(2,1)}), bf16[128,4,2048]{2,1,0:T(4,128)(2,1)}, u32[]{:S(2)}, u32[]{:S(2)}) async-start(bf16[128,4,2048]{2,1,0:T(4,128)(2,1)} %reshape.233), calls=%async_computation.2 | async-start | bytes 4194304 | tf_op jit(solution)/shard_map/all_to_all | solution.py:50
  105.0 29.7 %all-to-all-done.2 = bf16[128,4,2048]{2,1,0:T(4,128)(2,1)} async-done(((bf16[128,4,2048]{2,1,0:T(4,128)(2,1)}), bf16[128,4,2048]{2,1,0:T(4,128)(2,1)}, u32[]{:S(2)}, u32[]{:S(2)}) %all-to-all-start.2) | async-done | bytes 2097184 | tf_op jit(solution)/shard_map/all_to_all | solution.py:50
  134.7 4.2 %reshape.272 = f32[512,2048]{1,0:T(8,128)} reshape(bf16[128,4,2048]{2,1,0:T(4,128)(2,1)} %all-to-all-done.2) | data formatting | bytes 6291456 | tf_op jit(solution)/shard_map/convert_element_type | solution.py:21
  138.9 10.7 %scatter_custom_fusion.2 = f32[512,2048]{1,0:T(8,128)} fusion(s32[512]{0:T(512)S(1)} %bitcast.78, f32[512,2048]{1,0:T(8,128)} %reshape.272, f32[]{:T(128)} %constant.59.clone.1), kind=kCustom, calls=%fused_computation.14 | custom fusion | flops 1048576 | bytes 4194816 | tf_op jit(solution)/shard_map/scatter-add | solution.py:20
  149.6 2.8 %select_reduce_fusion = (f32[8,128]{1,0:T(8,128)S(1)}, f32[8,128,1024]{2,1,0:T(8,128)S(1)}) fusion(pred[128,1024]{1,0:T(8,128)(4,1)S(1)} %iota_compare_fusion, bf16[16,8,8,128]{3,2,1,0:T(8,128)(2,1)S(1)} %get-tuple-element.8, bf16[1024,1024]{1,0:T(8,128)(2,1)} %all-gather.3.cloned.1.call-done), kind=kOutput, calls=%fused_computation.6 | convolution fusion | flops 271580160 | bytes 6688768 | tf_op jit(solution)/shard_map/qhd,khd->hqk/dot_general | solution.py:68
  152.4 1.9 %copy-done.1 = f32[8,128,1024]{2,1,0:T(8,128)} copy-done((f32[8,128,1024]{2,1,0:T(8,128)}, f32[8,128,1024]{2,1,0:T(8,128)S(1)}, u32[]{:S(2)}) %copy-start.1) | copy-done | bytes 4194328
  154.3 1.2 fusion
  155.5 6.6 %all-gather.5.cloned.1.call-done = bf16[1024,1024]{1,0:T(8,128)(2,1)} async-done(((bf16[128,1024]{1,0:T(8,128)(2,1)}), bf16[1024,1024]{1,0:T(8,128)(2,1)}) %all-gather.5.cloned.1.call-update) | async-done | bytes 2097168 | tf_op jit(solution)/shard_map/all_gather | solution.py:63
  162.1 4.0 %copy.21 = bf16[1024,1024]{0,1:T(8,128)(2,1)} copy(bf16[1024,1024]{1,0:T(8,128)(2,1)} %all-gather.5.cloned.1.call-done) | data formatting | bytes 4194304 | tf_op jit(solution)/shard_map/reshape | solution.py:66
  166.0 4.0 %fusion.21 = bf16[128,8,128]{0,2,1:T(8,128)(2,1)S(1)} fusion(bf16[1024,8,128]{0,2,1:T(8,128)(2,1)} %bitcast.73, f32[8,128,1024]{2,1,0:T(8,128)} %copy-done.1, f32[8,128]{1,0:T(8,128)S(1)} %broadcast_maximum_fusion, pred[128,1024]{1,0:T(8,128)(4,1)S(1)} %iota_compare_fusion, f32[128,8]{0,1:T(8,128)S(1)} %bitcast.77), kind=kOutput, calls=%fused_computation.27 | convolution fusion | flops 272891904 | bytes 6692864 | tf_op jit(solution)/shard_map/hqk,khd->hqd/dot_general | solution.py:76
  170.0 0.9 copy.20
  (31 shorter events, 4.0 us)
Async XLA Ops:
  7.2 25.3 %copy-start = (bf16[512,2048]{1,0:T(8,128)(2,1)S(1)}, bf16[512,2048]{1,0:T(8,128)(2,1)}, u32[]{:S(2)}) copy-start(bf16[512,2048]{1,0:T(8,128)(2,1)} %param.8) | copy-start | bytes 6291460
  35.7 9.9 %copy-start.3 = (bf16[2048]{0:T(1024)(128)(2,1)S(1)}, bf16[2048]{0:T(1024)(128)(2,1)}, u32[]{:S(2)}) copy-start(bf16[2048]{0:T(1024)(128)(2,1)} %param.10) | copy-start | bytes 12292
  39.9 35.7 %all-to-all-start.1 = ((bf16[128,4,2048]{2,1,0:T(4,128)(2,1)}), bf16[128,4,2048]{2,1,0:T(4,128)(2,1)}, u32[]{:S(2)}, u32[]{:S(2)}) async-start(bf16[128,4,2048]{2,1,0:T(4,128)(2,1)} %reshape.237), calls=%async_computation.1 | async-start | bytes 4194304 | tf_op jit(solution)/shard_map/all_to_all | solution.py:12
  45.5 104.1 %all-gather.3.cloned.1.call-start = ((), (), s32[]{:S(2)}) async-start(), calls=%async_computation.3 | async-start | bytes 2359296 | tf_op jit(solution)/shard_map/all_gather | solution.py:62
  45.6 37.2 %copy-start.2 = (bf16[1,128,2048]{2,1,0:T(8,128)(2,1)S(1)}, bf16[1,128,2048]{2,1,0:T(8,128)(2,1)}, u32[]{:S(2)}) copy-start(bf16[1,128,2048]{2,1,0:T(8,128)(2,1)} %param.6) | copy-start | bytes 1572868
  90.5 71.6 %all-gather.5.cloned.1.call-start = ((), (), s32[]{:S(2)}) async-start(), calls=%async_computation.4 | async-start | bytes 2359296 | tf_op jit(solution)/shard_map/all_gather | solution.py:63
  98.9 35.8 %all-to-all-start.2 = ((bf16[128,4,2048]{2,1,0:T(4,128)(2,1)}), bf16[128,4,2048]{2,1,0:T(4,128)(2,1)}, u32[]{:S(2)}, u32[]{:S(2)}) async-start(bf16[128,4,2048]{2,1,0:T(4,128)(2,1)} %reshape.233), calls=%async_computation.2 | async-start | bytes 4194304 | tf_op jit(solution)/shard_map/all_to_all | solution.py:50
  152.4 1.9 %copy-start.1 = (f32[8,128,1024]{2,1,0:T(8,128)}, f32[8,128,1024]{2,1,0:T(8,128)S(1)}, u32[]{:S(2)}) copy-start(f32[8,128,1024]{2,1,0:T(8,128)S(1)} %get-tuple-element.16) | copy-start | bytes 12582916
Sparse Core Ops, SparseCore 0:
  90.6 38.8 all-gather.2
  131.8 30.2 all-gather.4
where the time goes:
time: 179 us; the launch traced here: 178 us
  waiting for transfers between devices  66.9 us (37%)
  local copies, waits for them, and re-layouts  35.9 us (20%)
  blocking collectives  20.7 us (12%)
  other arithmetic  15.1 us (8%)
  between operations  14.2 us (8%)
  matrix products  13.3 us (7%)
  starting transfers between devices  11.5 us (6%)
    all_to_all x1, waiting for transfers between devices, fetch_rows(): lax.all_to_all(rows, ('table', 'ctx'), split_axis=0, concat_axis=0, tiled...  29.9 us
    all_to_all x1, waiting for transfers between devices, shards(): lax.all_to_all(cot_slots, ('table', 'ctx'), split_axis=0, concat_axis=0,...  29.7 us
    all_to_all x1, blocking collectives, shards(): lax.all_to_all(requests, ('table', 'ctx'), split_axis=0, concat_axis=0, t...  20.7 us
    scatter-add x1, other arithmetic, add_grads(): grads.at[target]  10.7 us
    gather x2, local copies, waits for them, and re-layouts, fetch_rows(): rows = ngram_table[jnp.clip(asked, 0, ngram_table.shape[0] - 1)]  7.41 us
    all_gather x1, waiting for transfers between devices, shards(): value_piece = lax.all_gather(values, 'ctx', axis=0, tiled=True)  6.56 us
    dot_general x1, matrix products, shards(): jnp.dot(normed, w_qkv, preferred_element_type=jnp.float32)  6.49 us
    all_to_all x1, starting transfers between devices, shards(): lax.all_to_all(cot_slots, ('table', 'ctx'), split_axis=0, concat_axis=0,...  5.78 us
  transfers between devices with their start and end apart: 4, of which 3 were waited for; matrix products, arithmetic and copies ran while one was open for 15% of the time, Pallas kernels for 0%

commit v1 on v0

v1 whole, which is shorter than its diff:
```python
import functools

import jax
import jax.numpy as jnp
from jax import lax
from jax.experimental import pallas as pl
from jax.experimental.pallas import tpu as pltpu
from jax.sharding import PartitionSpec as P

HEAD = 128
HEADS = 8
CAP = 4
HALF = 1024
MB = 1024 * 1024


def iota(shape, dim):
    return lax.broadcasted_iota(jnp.int32, shape, dim)


def dot(a, b, dims=(((1,), (0,)), ((), ()))):
    return lax.dot_general(a, b, dims, preferred_element_type=jnp.float32)


def owner_grid(ids_ref, held):
    n = ids_ref.shape[1]
    ids = jnp.broadcast_to(ids_ref[...], (n, n))
    owner = ids // held
    return ids, owner, owner.astype(jnp.float32).T.astype(jnp.int32)


def pack_kernel(held, ids_ref, cot_ref, req_ref, send_ref):
    n = ids_ref.shape[1]
    ids, own_lane, own_sub = owner_grid(ids_ref, held)
    same = (own_lane == own_sub) & (iota((n, n), 0) < iota((n, n), 1))
    rank = jnp.sum(same.astype(jnp.int32), axis=0, keepdims=True)
    local = (ids - own_lane * held + 1).astype(jnp.float32)
    mine = own_lane == iota((n, n), 0)
    lane = iota((n, n), 1)
    req = jnp.zeros((n, n), jnp.float32)
    for c in range(CAP):
        found = jnp.sum(jnp.where(mine & (rank == c), local, 0.0), axis=1, keepdims=True)
        req = jnp.where(lane == c, found, req)
    req_ref[...] = req.astype(jnp.int32).reshape(n, 1, n)
    slot = own_lane[0:1] * (2 * CAP) + rank
    rows = iota((n * 2 * CAP, n), 0)
    low = (rows == slot).astype(jnp.bfloat16)
    high = (rows == slot + CAP).astype(jnp.bfloat16)
    send_ref[...] = (
        dot(low, cot_ref[:, :HALF]) + dot(high, cot_ref[:, HALF:])
    ).astype(jnp.bfloat16)


def slot_onehot(asked_ref, held):
    n = asked_ref.shape[0]
    wide = jnp.broadcast_to(asked_ref[...], (n, 2 * CAP, n)).reshape(n * 2 * CAP, n)
    rows = iota((n * 2 * CAP, n), 0) % (2 * CAP)
    lane = iota((n * 2 * CAP, n), 1)
    asked = jnp.sum(
        jnp.where(lane == rows % CAP, wide, 0).astype(jnp.float32), axis=1, keepdims=True
    ).astype(jnp.int32)
    hit = asked == iota((n * 2 * CAP, held), 1) + 1
    upper = iota((n * 2 * CAP, held), 0) % (2 * CAP) >= CAP
    low = jnp.where(hit & ~upper, 1.0, 0.0).astype(jnp.bfloat16)
    high = jnp.where(hit & upper, 1.0, 0.0).astype(jnp.bfloat16)
    return low, high


def rows_kernel(asked_ref, table_ref, send_ref):
    low, high = slot_onehot(asked_ref, table_ref.shape[0])
    send_ref[...] = (
        dot(low, table_ref[:, :HALF]) + dot(high, table_ref[:, HALF:])
    ).astype(jnp.bfloat16)


def grad_kernel(asked_ref, cot_ref, grad_ref):
    low, high = slot_onehot(asked_ref, grad_ref.shape[0])
    first = (((0,), (0,)), ((), ()))
    grad_ref[:, :HALF] = dot(low, cot_ref[...], first)
    grad_ref[:, HALF:] = dot(high, cot_ref[...], first)


def qkv_kernel(held, ids_ref, got_ref, base_ref, gain_ref, w_ref, out_ref, normed_ref):
    step = pl.program_id(0)

    @pl.when(step == 0)
    def _():
        n = ids_ref.shape[1]
        _, own_lane, own_sub = owner_grid(ids_ref, held)
        same = (own_lane == own_sub) & (iota((n, n), 1) < iota((n, n), 0))
        rank = jnp.sum(same.astype(jnp.int32), axis=1, keepdims=True)
        slot = own_sub[:, 0:1] * (2 * CAP) + rank
        rows = iota((n, n * 2 * CAP), 1)
        low = (rows == slot).astype(jnp.bfloat16)
        high = (rows == slot + CAP).astype(jnp.bfloat16)
        base = base_ref[...].astype(jnp.float32)
        sum_low = base[:, :HALF] + dot(low, got_ref[...])
        sum_high = base[:, HALF:] + dot(high, got_ref[...])
        square = jnp.sum(sum_low * sum_low, axis=1, keepdims=True) + jnp.sum(
            sum_high * sum_high, axis=1, keepdims=True
        )
        scale = lax.rsqrt(square * (1.0 / (2 * HALF)) + 1e-05)
        gain = gain_ref[...].astype(jnp.float32)
        normed_ref[:, :HALF] = (sum_low * scale * gain[:, :HALF]).astype(jnp.bfloat16)
        normed_ref[:, HALF:] = (sum_high * scale * gain[:, HALF:]).astype(jnp.bfloat16)

    heads = w_ref.shape[1] // HEAD
    made = dot(normed_ref[...], w_ref[...]).astype(jnp.bfloat16)
    for h in range(heads):
        out_ref[h] = made[:, h * HEAD : (h + 1) * HEAD]


def attention_kernel(block, qkv_ref, out_ref):
    seq = qkv_ref.shape[0]
    for i in range(seq // block):
        count = (i + 1) * block
        query = qkv_ref[i * block : count, :HEAD]
        keys = qkv_ref[:count, HEAD : 2 * HEAD]
        values = qkv_ref[:count, 2 * HEAD :]
        scores = dot(query, keys, (((1,), (1,)), ((), ()))) * HEAD ** (-0.5)
        allowed = iota((block, count), 1) <= iota((block, count), 0) + i * block
        scores = jnp.where(allowed, scores, -1e30)
        top = jnp.max(scores, axis=1, keepdims=True)
        weights = jnp.where(allowed, jnp.exp(scores - top), 0.0)
        total = jnp.sum(weights, axis=1, keepdims=True)
        mixed = dot(weights.astype(jnp.bfloat16), values)
        out_ref[i * block : count, :] = (mixed / total).astype(jnp.bfloat16)


def vmem(mb):
    return pltpu.CompilerParams(vmem_limit_bytes=mb * MB)


def cost(flops, moved):
    return pl.CostEstimate(flops=flops, bytes_accessed=moved, transcendentals=0)


def shards(base_embed, ngram_ids, ngram_table, embed_cot, norm_gain, w_qkv):
    tokens = ngram_ids.shape[1]
    width = base_embed.shape[2]
    held = ngram_table.shape[0]
    both = ("table", "ctx")
    owners = lax.axis_size("table") * lax.axis_size("ctx")
    ctx = lax.axis_size("ctx")
    slots = owners * 2 * CAP

    def exchange(x, axes=both):
        return lax.all_to_all(x, axes, split_axis=0, concat_axis=0, tiled=True)

    bf16, f32 = jnp.bfloat16, jnp.float32
    requests, cot_slots = pl.pallas_call(
        functools.partial(pack_kernel, held),
        out_shape=[
            jax.ShapeDtypeStruct((owners, 1, tokens), jnp.int32),
            jax.ShapeDtypeStruct((slots, HALF), bf16),
        ],
        compiler_params=vmem(24),
        cost_estimate=cost(2 * slots * tokens * width, 3 * MB),
        name="pack",
    )(ngram_ids, embed_cot[0])
    asked = exchange(requests)
    cot_all = exchange(cot_slots)
    row_slots = pl.pallas_call(
        rows_kernel,
        out_shape=jax.ShapeDtypeStruct((slots, HALF), bf16),
        compiler_params=vmem(24),
        cost_estimate=cost(2 * slots * held * width, 4 * MB),
        name="rows",
    )(asked, ngram_table)
    got = exchange(row_slots)
    table_grad = pl.pallas_call(
        grad_kernel,
        out_shape=jax.ShapeDtypeStruct((held, width), f32),
        compiler_params=vmem(24),
        cost_estimate=cost(2 * slots * held * width, 6 * MB),
        name="grad",
    )(asked, cot_all)
    columns = w_qkv.shape[1]
    blocks = 3 * 2
    per = columns // blocks
    heads_per = per // HEAD
    whole = lambda i: (0, 0)
    qkv = pl.pallas_call(
        functools.partial(qkv_kernel, held),
        grid=(blocks,),
        in_specs=[
            pl.BlockSpec((1, tokens), whole),
            pl.BlockSpec((slots, HALF), whole),
            pl.BlockSpec((tokens, width), whole),
            pl.BlockSpec((1, width), whole),
            pl.BlockSpec((width, per), lambda i: (0, i)),
        ],
        out_specs=pl.BlockSpec((heads_per, tokens, HEAD), lambda i: (i % 2, 0, i // 2)),
        out_shape=jax.ShapeDtypeStruct((ctx, tokens, 3 * HEAD), bf16),
        scratch_shapes=[pltpu.VMEM((tokens, width), bf16)],
        compiler_params=vmem(24),
        cost_estimate=cost(2 * tokens * width * columns, 16 * MB),
        name="qkv",
    )(ngram_ids, got, base_embed[0], norm_gain.reshape(1, width), w_qkv)
    mine = exchange(qkv, "ctx").reshape(ctx * tokens, 3 * HEAD)
    mixed = pl.pallas_call(
        functools.partial(attention_kernel, 256),
        out_shape=jax.ShapeDtypeStruct((ctx * tokens, HEAD), bf16),
        compiler_params=vmem(24),
        cost_estimate=cost(4 * ctx * tokens * ctx * tokens * HEAD, 2 * MB),
        name="attention",
    )(mine)
    context = exchange(mixed.reshape(ctx, tokens, HEAD), "ctx")
    context = context.transpose(1, 0, 2).reshape(tokens, HEADS * HEAD)
    return (context[None], table_grad)


def solution(mesh):
    return jax.shard_map(
        shards,
        mesh=mesh,
        in_specs=(
            P("table", "ctx", None),
            P("table", "ctx"),
            P(("table", "ctx"), None),
            P("table", "ctx", None),
            P(),
            P(),
        ),
        out_specs=(P("table", "ctx", None), P(("table", "ctx"), None)),
        check_vma=False,
    )
```

time: 179 us -> 138 us (0.77)
  local copies, waits for them, and re-layouts: 35.9 us -> 9.92 us
  Pallas kernels: 0 us -> 16 us
  blocking collectives: 20.7 us -> 36.6 us
  other arithmetic: 15.1 us -> 0 us
  between operations: 14.2 us -> 0.72 us
  matrix products: 13.3 us -> 0 us
  waiting for transfers between devices: 66.9 us -> 60.1 us
  starting transfers between devices: 11.5 us -> 13.8 us
    pallas_call x0 -> x5, Pallas kernels: none -> 16 us  [the longest x1 5.04 us: shards(): pl.pallas_call(functools.partial(qkv_kernel, held), grid=(blocks,), in_sp...]
    all_to_all x1 -> x2, blocking collectives: 20.7 us -> 36.6 us  [exchange(): return lax.all_to_all(x, axes, split_axis=0, concat_axis=0, tiled=True)]
    dot_general x3 -> x0, matrix products: 13.3 us -> none  [the longest x1 6.49 us: shards(): jnp.dot(normed, w_qkv, preferred_element_type=jnp.float32)]
    reshape x4 -> x1, local copies, waits for them, and re-layouts: 12.1 us -> 0.01 us  [shards(): norm_gain.reshape(1, width)]
    gather x3 -> x0, local copies, waits for them, and re-layouts: 10.7 us -> none  [the longest x2 7.41 us: fetch_rows(): rows = ngram_table[jnp.clip(asked, 0, ngram_table.shape[0] - 1)]]
    scatter-add x1 -> x0, other arithmetic: 10.7 us -> none  [add_grads(): grads.at[target]]
    all_gather x2 -> x0, waiting for transfers between devices: 6.56 us -> none  [the longest x1 6.56 us: shards(): value_piece = lax.all_gather(values, 'ctx', axis=0, tiled=True)]
    unnamed x10 -> x18, local copies, waits for them, and re-layouts: 3.64 us -> 8.92 us
  transfers between devices with their start and end apart: 4 -> 3, of which waited for: 3 -> 3; matrix products, arithmetic and copies ran while one was open for 15% -> 0% of each run, Pallas kernels for 0% -> 5%
where the time goes in v1:
time: 138 us; the launch traced here: 137 us
  waiting for transfers between devices  60.1 us (44%)
  blocking collectives  36.6 us (27%)
  Pallas kernels  16 us (12%)
  starting transfers between devices  13.8 us (10%)
  local copies, waits for them, and re-layouts  9.92 us (7%)
    all_to_all x3, waiting for transfers between devices, exchange(): return lax.all_to_all(x, axes, split_axis=0, concat_axis=0, tiled=True)  60.1 us
    all_to_all x2, blocking collectives, exchange(): return lax.all_to_all(x, axes, split_axis=0, concat_axis=0, tiled=True)  36.6 us
    all_to_all x3, starting transfers between devices, exchange(): return lax.all_to_all(x, axes, split_axis=0, concat_axis=0, tiled=True)  13.8 us
    unnamed x18, local copies, waits for them, and re-layouts  8.92 us
    pallas_call x1, Pallas kernels, shards(): pl.pallas_call(functools.partial(qkv_kernel, held), grid=(blocks,), in_sp...  5.04 us
    pallas_call x1, Pallas kernels, shards(): pl.pallas_call(grad_kernel, out_shape=jax.ShapeDtypeStruct((held, width),...  4.66 us
  transfers between devices with their start and end apart: 3, of which 3 were waited for; matrix products, arithmetic and copies ran while one was open for 0% of the time, Pallas kernels for 5%

profile of v1, /device:TPU:1, one launch (start us, length us, event | category | flops | bytes accessed | tf_op | source)
XLA Modules:
  0.0 137.2 jit_solution(2169207978492381200)
XLA Ops:
  0.6 0.0 copy-start.4
  0.6 0.6 copy-done.4
  1.3 1.0 copy-done.7
  2.3 1.4 %pack.1 = (s32[128,1,128]{2,1,0:T(1,128)S(1)}, bf16[1024,1024]{1,0:T(8,128)(2,1)S(1)}) custom-call(s32[1,128]{1,0:T(1,128)S(1)} %copy-done.4, bf16[128,2048]{1,0:T(8,128)(2,1)S(1)} %bitcast.15), custom_call_target="tpu_custom_call" | custom-call | flops 536870912 | bytes 3145728 | tf_op jit(solution)/shard_map/pack/pallas_call | solution.py:151
  3.7 0.0 copy-start.1
  3.7 1.3 copy-done.1
  5.1 20.7 %all_to_all.37.asked_ref = s32[128,1,128]{2,1,0:T(1,128)S(1)} all-to-all(s32[128,1,128]{2,1,0:T(1,128)S(1)} %get-tuple-element.4), channel_id=1, replica_groups=mesh['table'=16,'ctx'=8] {'table','ctx'}, dimensions={0} | all-to-all | bytes 131072 | tf_op jit(solution)/shard_map/all_to_all | solution.py:148
  25.8 2.5 %rows.1 = bf16[1024,1024]{1,0:T(8,128)(2,1)S(1)} custom-call(s32[128,1,128]{2,1,0:T(1,128)S(1)} %all_to_all.37.asked_ref, bf16[512,2048]{1,0:T(8,128)(2,1)S(1)} %copy-done.6), custom_call_target="tpu_custom_call" | custom-call | flops 2147483648 | bytes 4194304 | tf_op jit(solution)/shard_map/rows/pallas_call | solution.py:163
  28.2 0.0 copy-start.2
  28.2 1.3 copy-done.2
  29.5 4.7 %all-to-all-start.1 = ((bf16[128,8,1024]{2,1,0:T(8,128)(2,1)}), bf16[128,8,1024]{2,1,0:T(8,128)(2,1)S(1)}, u32[]{:S(2)}, u32[]{:S(2)}) async-start(bf16[128,8,1024]{2,1,0:T(8,128)(2,1)} %bitcast.12), calls=%async_computation.1 | async-start | bytes 4194304 | tf_op jit(solution)/shard_map/all_to_all | solution.py:148
  34.3 30.4 %all-to-all-done.1 = bf16[128,8,1024]{2,1,0:T(8,128)(2,1)S(1)} async-done(((bf16[128,8,1024]{2,1,0:T(8,128)(2,1)}), bf16[128,8,1024]{2,1,0:T(8,128)(2,1)S(1)}, u32[]{:S(2)}, u32[]{:S(2)}) %all-to-all-start.1) | async-done | bytes 2097184 | tf_op jit(solution)/shard_map/all_to_all | solution.py:148
  64.7 0.0 copy-done.3
  64.7 4.6 %copy-done = bf16[2048,3072]{1,0:T(8,128)(2,1)S(1)} copy-done((bf16[2048,3072]{1,0:T(8,128)(2,1)S(1)}, bf16[2048,3072]{1,0:T(8,128)(2,1)}, u32[]{:S(2)}) %copy-start) | copy-done | bytes 12582936
  69.3 5.0 %qkv.1 = bf16[8,128,384]{2,1,0:T(8,128)(2,1)S(1)} custom-call(s32[1,128]{1,0:T(1,128)S(1)} %copy-done.5, bf16[1024,1024]{1,0:T(8,128)(2,1)S(1)} %bitcast.9, bf16[128,2048]{1,0:T(8,128)(2,1)S(1)} %bitcast.14, bf16[1,2048]{1,0:T(2,128)(2,1)S(1)} %reshape.17.gain_ref, bf16[2048,3072]{1,0:T(8,128)(2,1)S(1)} %copy-done), custom_call_target="tpu_custom_call" | custom-call | flops 1610612736 | bytes 16777216 | tf_op jit(solution)/shard_map/qkv/pallas_call | solution.py:183
  74.3 15.9 %all_to_all.38 = bf16[8,128,384]{2,1,0:T(8,128)(2,1)S(1)} all-to-all(bf16[8,128,384]{2,1,0:T(8,128)(2,1)S(1)} %qkv.1), channel_id=1, replica_groups=mesh['table'=16,'ctx'=8] {'ctx'}, dimensions={0} | all-to-all | bytes 1572864 | tf_op jit(solution)/shard_map/all_to_all | solution.py:148
  90.2 4.5 %all-to-all-start.4 = ((bf16[128,8,1024]{2,1,0:T(8,128)(2,1)}), bf16[128,8,1024]{2,1,0:T(8,128)(2,1)S(1)}, u32[]{:S(2)}, u32[]{:S(2)}) async-start(bf16[128,8,1024]{2,1,0:T(8,128)(2,1)} %bitcast.10), calls=%async_computation.4 | async-start | bytes 4194304 | tf_op jit(solution)/shard_map/all_to_all | solution.py:148
  94.7 2.5 %attention.1 = bf16[1024,128]{1,0:T(8,128)(2,1)} custom-call(bf16[1024,384]{1,0:T(8,128)(2,1)S(1)} %bitcast.13), custom_call_target="tpu_custom_call" | custom-call | flops 536870912 | bytes 2097152 | tf_op jit(solution)/shard_map/attention/pallas_call | solution.py:201
  97.2 27.9 %all-to-all-done.4 = bf16[128,8,1024]{2,1,0:T(8,128)(2,1)S(1)} async-done(((bf16[128,8,1024]{2,1,0:T(8,128)(2,1)}), bf16[128,8,1024]{2,1,0:T(8,128)(2,1)S(1)}, u32[]{:S(2)}, u32[]{:S(2)}) %all-to-all-start.4) | async-done | bytes 2097184 | tf_op jit(solution)/shard_map/all_to_all | solution.py:148
  125.1 4.6 %all-to-all-start.3 = ((bf16[8,128,128]{2,1,0:T(8,128)(2,1)}), bf16[8,128,128]{2,1,0:T(8,128)(2,1)S(1)}, u32[]{:S(2)}, u32[]{:S(2)}) async-start(bf16[8,128,128]{2,1,0:T(8,128)(2,1)} %bitcast.5), calls=%async_computation.3 | async-start | bytes 524288 | tf_op jit(solution)/shard_map/all_to_all | solution.py:148
  129.7 4.7 %grad.1 = f32[512,2048]{1,0:T(8,128)} custom-call(s32[128,1,128]{2,1,0:T(1,128)S(1)} %all_to_all.37.asked_ref, bf16[1024,1024]{1,0:T(8,128)(2,1)S(1)} %bitcast.11), custom_call_target="tpu_custom_call" | custom-call | flops 2147483648 | bytes 6291456 | tf_op jit(solution)/shard_map/grad/pallas_call | solution.py:171
  134.3 1.9 %all-to-all-done.3 = bf16[8,128,128]{2,1,0:T(8,128)(2,1)S(1)} async-done(((bf16[8,128,128]{2,1,0:T(8,128)(2,1)}), bf16[8,128,128]{2,1,0:T(8,128)(2,1)S(1)}, u32[]{:S(2)}, u32[]{:S(2)}) %all-to-all-start.3) | async-done | bytes 262176 | tf_op jit(solution)/shard_map/all_to_all | solution.py:148
  136.2 0.2 copy.8
  136.4 0.8 broadcast_in_dim_reshape.3
  (10 shorter events, 0.0 us)
Async XLA Ops:
  0.6 0.7 copy-start.4
  1.3 1.0 copy-start.7
  2.3 23.4 %copy-start.6 = (bf16[512,2048]{1,0:T(8,128)(2,1)S(1)}, bf16[512,2048]{1,0:T(8,128)(2,1)}, u32[]{:S(2)}) copy-start(bf16[512,2048]{1,0:T(8,128)(2,1)} %table_ref.1) | copy-start | bytes 6291460
  3.7 1.3 copy-start.1
  28.2 1.3 copy-start.2
  29.5 4.8 %copy-start.8 = (bf16[2048]{0:T(1024)(128)(2,1)S(1)}, bf16[2048]{0:T(1024)(128)(2,1)}, u32[]{:S(2)}) copy-start(bf16[2048]{0:T(1024)(128)(2,1)} %param.10) | copy-start | bytes 12292
  29.5 35.1 %copy-start.3 = (bf16[1,128,2048]{2,1,0:T(8,128)(2,1)S(1)}, bf16[1,128,2048]{2,1,0:T(8,128)(2,1)}, u32[]{:S(2)}) copy-start(bf16[1,128,2048]{2,1,0:T(8,128)(2,1)} %param.6) | copy-start | bytes 1572868
  29.5 35.1 %copy-start.5 = (s32[1,128]{1,0:T(1,128)S(1)}, s32[1,128]{1,0:T(1,128)}, u32[]{:S(2)}) copy-start(s32[1,128]{1,0:T(1,128)} %ids_ref.3) | copy-start | bytes 1540
  29.5 35.1 %all-to-all-start.1 = ((bf16[128,8,1024]{2,1,0:T(8,128)(2,1)}), bf16[128,8,1024]{2,1,0:T(8,128)(2,1)S(1)}, u32[]{:S(2)}, u32[]{:S(2)}) async-start(bf16[128,8,1024]{2,1,0:T(8,128)(2,1)} %bitcast.12), calls=%async_computation.1 | async-start | bytes 4194304 | tf_op jit(solution)/shard_map/all_to_all | solution.py:148
  64.7 4.6 %copy-start = (bf16[2048,3072]{1,0:T(8,128)(2,1)S(1)}, bf16[2048,3072]{1,0:T(8,128)(2,1)}, u32[]{:S(2)}) copy-start(bf16[2048,3072]{1,0:T(8,128)(2,1)} %w_ref.1) | copy-start | bytes 37748740
  90.2 34.9 %all-to-all-start.4 = ((bf16[128,8,1024]{2,1,0:T(8,128)(2,1)}), bf16[128,8,1024]{2,1,0:T(8,128)(2,1)S(1)}, u32[]{:S(2)}, u32[]{:S(2)}) async-start(bf16[128,8,1024]{2,1,0:T(8,128)(2,1)} %bitcast.10), calls=%async_computation.4 | async-start | bytes 4194304 | tf_op jit(solution)/shard_map/all_to_all | solution.py:148
  125.1 11.1 %all-to-all-start.3 = ((bf16[8,128,128]{2,1,0:T(8,128)(2,1)}), bf16[8,128,128]{2,1,0:T(8,128)(2,1)S(1)}, u32[]{:S(2)}, u32[]{:S(2)}) async-start(bf16[8,128,128]{2,1,0:T(8,128)(2,1)} %bitcast.5), calls=%async_computation.3 | async-start | bytes 524288 | tf_op jit(solution)/shard_map/all_to_all | solution.py:148

commit v2 on v0

v2 whole, which is shorter than its diff:
```python
import functools

import jax
import jax.numpy as jnp
from jax import lax
from jax.experimental import pallas as pl
from jax.experimental.pallas import tpu as pltpu
from jax.sharding import PartitionSpec as P

HEAD = 128
HEADS = 8
CAP = 4
TILE = 2 * CAP
HALF = 1024
MB = 1024 * 1024
BOTH = ("table", "ctx")


def iota(shape, dim):
    return lax.broadcasted_iota(jnp.int32, shape, dim)


def dot(a, b, dims=(((1,), (0,)), ((), ()))):
    return lax.dot_general(a, b, dims, preferred_element_type=jnp.float32)


def onehot(mask):
    return jnp.where(mask, 1.0, 0.0).astype(jnp.bfloat16)


def owner_grid(ids, held):
    n = ids.shape[1]
    owner = jnp.broadcast_to(ids, (n, n)) // held
    return owner, owner.astype(jnp.float32).T.astype(jnp.int32)


def asked_rows(ids_ref, held):
    n, _, tokens = ids_ref.shape
    me = lax.axis_index("table") * lax.axis_size("ctx") + lax.axis_index("ctx")
    wide = jnp.broadcast_to(ids_ref[...], (n, TILE, tokens)).reshape(n * TILE, tokens)
    local = wide - me * held
    mine = (local >= 0) & (local < held)
    earlier = onehot(iota((tokens, tokens), 0) < iota((tokens, tokens), 1))
    rank = dot(onehot(mine), earlier)
    slot = (iota(wide.shape, 0) % CAP).astype(jnp.float32)
    return jnp.where(mine & (rank == slot), local + 1, 0)


def rows_kernel(ids_ref, table_ref, send_ref):
    held = table_ref.shape[0]
    asked = asked_rows(ids_ref, held)
    row = jnp.sum(asked.astype(jnp.float32), axis=1, keepdims=True).astype(jnp.int32)
    shape = (row.shape[0], held)
    hit = row == iota(shape, 1) + 1
    upper = iota(shape, 0) % TILE >= CAP
    send_ref[...] = (
        dot(onehot(hit & ~upper), table_ref[:, :HALF])
        + dot(onehot(hit & upper), table_ref[:, HALF:])
    ).astype(jnp.bfloat16)


def cot_kernel(held, ids_ref, cot_ref, send_ref):
    ctx = lax.axis_size("ctx")
    tokens = ids_ref.shape[2]
    rows = send_ref.shape[0] * TILE
    first = lax.axis_index("table") * ctx
    for src in range(ctx):
        own_lane, own_sub = owner_grid(ids_ref[first + src], held)
        earlier = iota((tokens, tokens), 0) < iota((tokens, tokens), 1)
        same = jnp.where((own_lane == own_sub) & earlier, 1, 0)
        rank = jnp.sum(same, axis=0, keepdims=True)
        owner = own_lane[0:1]
        slot = jnp.where(owner % ctx == lax.axis_index("ctx"), owner // ctx * TILE + rank, -TILE)
        at = iota((rows, tokens), 0)
        cot = cot_ref.at[src * tokens : (src + 1) * tokens]
        made = dot(onehot(at == slot), cot[:, :HALF]) + dot(onehot(at == slot + CAP), cot[:, HALF:])
        send_ref[:, src * TILE : (src + 1) * TILE, :] = made.astype(jnp.bfloat16).reshape(
            rows // TILE, TILE, HALF
        )


def grad_kernel(ids_ref, cot_ref, grad_ref, low_ref, high_ref):
    held = grad_ref.shape[0]
    step = pl.program_id(0)
    half = pl.num_programs(0) // 2

    @pl.when(step == 0)
    def _():
        asked = asked_rows(ids_ref, held)
        lanes = (((1,), (1,)), ((), ()))
        ones = jnp.ones((8, asked.shape[1]), jnp.bfloat16)
        top = asked // 256
        row = 256.0 * dot(ones, top.astype(jnp.float32).astype(jnp.bfloat16), lanes) + dot(
            ones, (asked - top * 256).astype(jnp.float32).astype(jnp.bfloat16), lanes
        )
        shape = low_ref.shape
        hit = row[0:1].astype(jnp.int32) == iota(shape, 0) + 1
        upper = iota(shape, 1) % TILE >= CAP
        low_ref[...] = onehot(hit & ~upper)
        high_ref[...] = onehot(hit & upper)

    @pl.when(step < half)
    def _():
        grad_ref[...] = dot(low_ref[...], cot_ref[...])

    @pl.when(step >= half)
    def _():
        grad_ref[...] = dot(high_ref[...], cot_ref[...])


def qkv_kernel(held, ids_ref, got_ref, base_ref, gain_ref, w_hbm, *refs):
    out_refs, (w_ref, normed_ref, made_ref, sems) = refs[:HEADS], refs[HEADS:]
    blocks, _, per = w_ref.shape
    copies = [
        pltpu.make_async_copy(w_hbm.at[:, j * per : (j + 1) * per], w_ref.at[j], sems.at[j])
        for j in range(blocks)
    ]
    for copy in copies:
        copy.start()
    n = ids_ref.shape[1]
    own_lane, own_sub = owner_grid(ids_ref[...], held)
    same = (own_lane == own_sub) & (iota((n, n), 1) < iota((n, n), 0))
    rank = jnp.sum(jnp.where(same, 1, 0), axis=1, keepdims=True)
    slot = own_sub[:, 0:1] * TILE + rank
    at = iota((n, got_ref.shape[0]), 1)
    base = base_ref[...].astype(jnp.float32)
    low = base[:, :HALF] + dot(onehot(at == slot), got_ref[...])
    high = base[:, HALF:] + dot(onehot(at == slot + CAP), got_ref[...])
    square = jnp.sum(low * low, axis=1, keepdims=True) + jnp.sum(high * high, axis=1, keepdims=True)
    scale = lax.rsqrt(square * (1.0 / (2 * HALF)) + 1e-05)
    gain = gain_ref[...].astype(jnp.float32)
    normed_ref[:, :HALF] = (low * scale * gain[:, :HALF]).astype(jnp.bfloat16)
    normed_ref[:, HALF:] = (high * scale * gain[:, HALF:]).astype(jnp.bfloat16)
    for j, copy in enumerate(copies):
        copy.wait()
        made = dot(normed_ref[...], w_ref[j]).astype(jnp.bfloat16)
        for i in range(per // HEAD):
            kind, head = divmod(j * per // HEAD + i, HEADS)
            made_ref[head, :, kind * HEAD : (kind + 1) * HEAD] = made[:, i * HEAD : (i + 1) * HEAD]
    me = lax.axis_index("ctx")
    for shift, ref in enumerate(out_refs):
        ref[...] = made_ref[(me + shift) % HEADS]


def attention_kernel(block, *refs):
    ins, outs, (qkv_ref, mixed_ref) = refs[:HEADS], refs[HEADS : 2 * HEADS], refs[2 * HEADS :]
    tokens = ins[0].shape[0]
    seq = tokens * HEADS
    me = lax.axis_index("ctx")
    for shift, ref in enumerate(ins):
        source = (me + HEADS - shift) % HEADS
        qkv_ref[pl.ds(pl.multiple_of(source * tokens, tokens), tokens), :] = ref[...]
    for i in range(seq // block):
        count = (i + 1) * block
        query = qkv_ref[i * block : count, :HEAD]
        keys = qkv_ref[:count, HEAD : 2 * HEAD]
        values = qkv_ref[:count, 2 * HEAD :]
        scores = dot(query, keys, (((1,), (1,)), ((), ()))) * HEAD ** (-0.5)
        allowed = iota((block, count), 1) <= iota((block, count), 0) + i * block
        scores = jnp.where(allowed, scores, -1e30)
        top = jnp.max(scores, axis=1, keepdims=True)
        weights = jnp.where(allowed, jnp.exp(scores - top), 0.0)
        total = jnp.sum(weights, axis=1, keepdims=True)
        mixed = dot(weights.astype(jnp.bfloat16), values)
        mixed_ref[i * block : count, :] = (mixed / total).astype(jnp.bfloat16)
    for shift, ref in enumerate(outs):
        target = (me + shift) % HEADS
        ref[...] = mixed_ref[pl.ds(pl.multiple_of(target * tokens, tokens), tokens), :]


def join_kernel(*refs):
    ins, out_ref = refs[:HEADS], refs[HEADS]
    me = lax.axis_index("ctx")
    for shift, ref in enumerate(ins):
        head = (me + HEADS - shift) % HEADS
        out_ref[:, pl.ds(pl.multiple_of(head * HEAD, HEAD), HEAD)] = ref[...]


def call(kernel, out, flops, moved, mb=24, **kwargs):
    return pl.pallas_call(
        kernel,
        out_shape=out,
        compiler_params=pltpu.CompilerParams(vmem_limit_bytes=mb * MB),
        cost_estimate=pl.CostEstimate(flops=flops, bytes_accessed=moved, transcendentals=0),
        **kwargs,
    )


def exchange(x, axes):
    return lax.all_to_all(x, axes, split_axis=0, concat_axis=0, tiled=True)


def shift_all(pieces):
    n = len(pieces)
    moved = [
        lax.ppermute(pieces[k], "ctx", [(i, (i + k) % n) for i in range(n)]) for k in range(1, n)
    ]
    return [pieces[0], *moved]


def shards(base_embed, ngram_ids, ngram_table, embed_cot, norm_gain, w_qkv):
    tokens = ngram_ids.shape[1]
    width = base_embed.shape[2]
    held = ngram_table.shape[0]
    table = lax.axis_size("table")
    ctx = lax.axis_size("ctx")
    owners = table * ctx
    slots = owners * TILE
    columns = w_qkv.shape[1]
    bf16, f32 = jnp.bfloat16, jnp.float32
    shape = jax.ShapeDtypeStruct

    all_ids = exchange(jnp.broadcast_to(ngram_ids[None], (owners, 1, tokens)), BOTH)
    seq_cot = lax.all_gather(embed_cot[0], "ctx", axis=0, tiled=True)
    row_slots = call(
        rows_kernel,
        shape((slots, HALF), bf16),
        2 * slots * held * width,
        4 * MB,
        name="rows",
    )(all_ids, ngram_table)
    got = exchange(row_slots, BOTH)
    cot_slots = call(
        functools.partial(cot_kernel, held),
        shape((table, ctx * TILE, HALF), bf16),
        2 * slots * tokens * width,
        6 * MB,
        name="cot_slots",
    )(all_ids, seq_cot)
    cot_all = exchange(cot_slots, "table").reshape(slots, HALF)
    blocks = 4
    per = width // blocks
    table_grad = call(
        grad_kernel,
        shape((held, width), f32),
        2 * slots * held * width,
        6 * MB,
        name="grad",
        grid=(blocks,),
        in_specs=[
            pl.BlockSpec((owners, 1, tokens), lambda j: (0, 0, 0)),
            pl.BlockSpec((slots, per), lambda j: (0, j % 2)),
        ],
        out_specs=pl.BlockSpec((held, per), lambda j: (0, j)),
        scratch_shapes=[pltpu.VMEM((held, slots), bf16)] * 2,
    )(all_ids, cot_all)
    blocks = 6
    whole = pl.BlockSpec(memory_space=pltpu.VMEM)
    qkv = call(
        functools.partial(qkv_kernel, held),
        [shape((tokens, 3 * HEAD), bf16)] * HEADS,
        2 * tokens * width * columns,
        16 * MB,
        mb=32,
        name="qkv",
        in_specs=[whole] * 4 + [pl.BlockSpec(memory_space=pltpu.HBM)],
        scratch_shapes=[
            pltpu.VMEM((blocks, width, columns // blocks), bf16),
            pltpu.VMEM((tokens, width), bf16),
            pltpu.VMEM((HEADS, tokens, 3 * HEAD), bf16),
            pltpu.SemaphoreType.DMA((blocks,)),
        ],
    )(ngram_ids, got, base_embed[0], norm_gain.reshape(1, width), w_qkv)
    mixed = call(
        functools.partial(attention_kernel, 256),
        [shape((tokens, HEAD), bf16)] * HEADS,
        4 * ctx * tokens * ctx * tokens * HEAD,
        2 * MB,
        name="attention",
        scratch_shapes=[
            pltpu.VMEM((ctx * tokens, 3 * HEAD), bf16),
            pltpu.VMEM((ctx * tokens, HEAD), bf16),
        ],
    )(*shift_all(qkv))
    context = call(
        join_kernel, shape((tokens, HEADS * HEAD), bf16), 0, MB // 2, name="join"
    )(*shift_all(mixed))
    return (context[None], table_grad)


def solution(mesh):
    return jax.shard_map(
        shards,
        mesh=mesh,
        in_specs=(
            P("table", "ctx", None),
            P("table", "ctx"),
            P(("table", "ctx"), None),
            P("table", "ctx", None),
            P(),
            P(),
        ),
        out_specs=(P("table", "ctx", None), P(("table", "ctx"), None)),
        check_vma=False,
    )
```

time: 179 us -> 133 us (0.74)
  waiting for transfers between devices: 66.9 us -> 40.3 us
  local copies, waits for them, and re-layouts: 35.9 us -> 10.4 us
  Pallas kernels: 0 us -> 20.9 us
  other arithmetic: 15.1 us -> 0 us
  starting transfers between devices: 11.5 us -> 26.3 us
  matrix products: 13.3 us -> 0 us
    all_to_all x2, waiting for transfers between devices: 59.7 us -> 16 us  [exchange(): return lax.all_to_all(x, axes, split_axis=0, concat_axis=0, tiled=True)]
    pallas_call x0 -> x6, Pallas kernels: none -> 20.9 us  [the longest x1 7.33 us: shards(): call(grad_kernel, shape((held, width), f32), 2 * slots * held * width, 6...]
    ppermute x0 -> x14, waiting for transfers between devices: none -> 14.1 us  [shift_all(): lax.ppermute(pieces[k], 'ctx', [(i, (i + k) % n) for i in range(n)])]
    dot_general x3 -> x0, matrix products: 13.3 us -> none  [the longest x1 6.49 us: shards(): jnp.dot(normed, w_qkv, preferred_element_type=jnp.float32)]
    ppermute x0 -> x14, starting transfers between devices: none -> 13.2 us  [shift_all(): lax.ppermute(pieces[k], 'ctx', [(i, (i + k) % n) for i in range(n)])]
    reshape x4 -> x1, local copies, waits for them, and re-layouts: 12.1 us -> 0.01 us  [shards(): norm_gain.reshape(1, width)]
    gather x3 -> x0, local copies, waits for them, and re-layouts: 10.7 us -> none  [the longest x2 7.41 us: fetch_rows(): rows = ngram_table[jnp.clip(asked, 0, ngram_table.shape[0] - 1)]]
    scatter-add x1 -> x0, other arithmetic: 10.7 us -> none  [add_grads(): grads.at[target]]
  transfers between devices with their start and end apart: 4 -> 17, of which waited for: 3 -> 8; matrix products, arithmetic and copies ran while one was open for 15% -> 1% of each run, Pallas kernels for 0% -> 10%
where the time goes in v2:
time: 133 us
  waiting for transfers between devices  40.3 us (30%)
  starting transfers between devices  26.3 us (20%)
  Pallas kernels  20.9 us (16%)
  blocking collectives  20.7 us (16%)
  between operations  14.1 us (11%)
  local copies, waits for them, and re-layouts  10.4 us (8%)
    all_to_all x1, blocking collectives, exchange(): return lax.all_to_all(x, axes, split_axis=0, concat_axis=0, tiled=True)  20.7 us
    all_to_all x2, waiting for transfers between devices, exchange(): return lax.all_to_all(x, axes, split_axis=0, concat_axis=0, tiled=True)  16 us
    ppermute x14, waiting for transfers between devices, shift_all(): lax.ppermute(pieces[k], 'ctx', [(i, (i + k) % n) for i in range(n)])  14.1 us
    ppermute x14, starting transfers between devices, shift_all(): lax.ppermute(pieces[k], 'ctx', [(i, (i + k) % n) for i in range(n)])  13.2 us
    all_to_all x2, starting transfers between devices, exchange(): return lax.all_to_all(x, axes, split_axis=0, concat_axis=0, tiled=True)  13 us
    unnamed x14, local copies, waits for them, and re-layouts  9.69 us
    all_gather x1, waiting for transfers between devices, shards(): seq_cot = lax.all_gather(embed_cot[0], 'ctx', axis=0, tiled=True)  9.5 us
    pallas_call x1, Pallas kernels, shards(): call(grad_kernel, shape((held, width), f32), 2 * slots * held * width, 6...  7.33 us
  transfers between devices with their start and end apart: 17, of which 8 were waited for; matrix products, arithmetic and copies ran while one was open for 1% of the time, Pallas kernels for 10%

profile of v2, /device:TPU:1, one launch (start us, length us, event | category | flops | bytes accessed | tf_op | source)
XLA Modules:
  0.0 132.7 jit_solution(11842738376822751230)
XLA Ops:
  8.6 20.7 %all_to_all.21.ids_ref = s32[128,1,128]{2,1,0:T(1,128)S(1)} all-to-all(s32[128,1,128]{2,1,0:T(1,128)S(1)} %broadcast_in_dim.12), channel_id=1, replica_groups=mesh['table'=16,'ctx'=8] {'table','ctx'}, dimensions={0} | all-to-all | bytes 131072 | tf_op jit(solution)/shard_map/all_to_all | solution.py:190
  29.3 1.6 %copy-done.5 = bf16[512,2048]{1,0:T(8,128)(2,1)S(1)} copy-done((bf16[512,2048]{1,0:T(8,128)(2,1)S(1)}, bf16[512,2048]{1,0:T(8,128)(2,1)}, u32[]{:S(2)}) %copy-start.5) | copy-done | bytes 2097176
  30.9 2.7 %rows.1 = bf16[1024,1024]{1,0:T(8,128)(2,1)S(1)} custom-call(s32[128,1,128]{2,1,0:T(1,128)S(1)} %all_to_all.21.ids_ref, bf16[512,2048]{1,0:T(8,128)(2,1)S(1)} %copy-done.5), custom_call_target="tpu_custom_call" | custom-call | flops 2147483648 | bytes 4194304 | tf_op jit(solution)/shard_map/rows/pallas_call | solution.py:215
  33.6 1.3 copy-done.2
  34.9 4.6 %all-to-all-start.1 = ((bf16[128,8,1024]{2,1,0:T(8,128)(2,1)}), bf16[128,8,1024]{2,1,0:T(8,128)(2,1)S(1)}, u32[]{:S(2)}, u32[]{:S(2)}) async-start(bf16[128,8,1024]{2,1,0:T(8,128)(2,1)} %bitcast.9), calls=%async_computation.1 | async-start | bytes 4194304 | tf_op jit(solution)/shard_map/all_to_all | solution.py:190
  39.5 9.5 %all-gather.3.cloned.1.call-done = bf16[1,1024,2048]{2,1,0:T(8,128)(2,1)} async-done(((bf16[1,128,2048]{2,1,0:T(8,128)(2,1)}), bf16[1,1024,2048]{2,1,0:T(8,128)(2,1)}) %all-gather.3.cloned.1.call-update) | async-done | bytes 4194320 | tf_op jit(solution)/shard_map/all_gather | solution.py:214
  49.0 2.2 %copy-done.1 = bf16[1,1024,2048]{2,1,0:T(8,128)(2,1)S(1)} copy-done((bf16[1,1024,2048]{2,1,0:T(8,128)(2,1)S(1)}, bf16[1,1024,2048]{2,1,0:T(8,128)(2,1)}, u32[]{:S(2)}) %copy-start.1) | copy-done | bytes 4194328
  51.2 2.7 %cot_slots.1 = bf16[16,64,1024]{2,1,0:T(8,128)(2,1)} custom-call(s32[128,1,128]{2,1,0:T(1,128)S(1)} %all_to_all.21.ids_ref, bf16[1024,2048]{1,0:T(8,128)(2,1)S(1)} %bitcast.8), custom_call_target="tpu_custom_call" | custom-call | flops 536870912 | bytes 6291456 | tf_op jit(solution)/shard_map/cot_slots/pallas_call | solution.py:223
  53.9 16.0 %all-to-all-done.1 = bf16[128,8,1024]{2,1,0:T(8,128)(2,1)S(1)} async-done(((bf16[128,8,1024]{2,1,0:T(8,128)(2,1)}), bf16[128,8,1024]{2,1,0:T(8,128)(2,1)S(1)}, u32[]{:S(2)}, u32[]{:S(2)}) %all-to-all-start.1) | async-done | bytes 2097184 | tf_op jit(solution)/shard_map/all_to_all | solution.py:190
  69.9 8.4 %all-to-all-start.2 = ((bf16[16,64,1024]{2,1,0:T(8,128)(2,1)}), bf16[16,64,1024]{2,1,0:T(8,128)(2,1)}, u32[]{:S(2)}, u32[]{:S(2)}) async-start(bf16[16,64,1024]{2,1,0:T(8,128)(2,1)} %cot_slots.1), calls=%async_computation.2 | async-start | bytes 4194304 | tf_op jit(solution)/shard_map/all_to_all | solution.py:190
  78.4 4.6 %copy-done = bf16[2048,3072]{1,0:T(8,128)(2,1)S(1)} copy-done((bf16[2048,3072]{1,0:T(8,128)(2,1)S(1)}, bf16[2048,3072]{1,0:T(8,128)(2,1)}, u32[]{:S(2)}) %copy-start) | copy-done | bytes 12582936
  83.0 5.5 %qkv.1 = (bf16[128,384]{1,0:T(8,128)(2,1)S(1)}, bf16[128,384]{1,0:T(8,128)(2,1)S(1)}, bf16[128,384]{1,0:T(8,128)(2,1)S(1)}, bf16[128,384]{1,0:T(8,128)(2,1)S(1)}...) custom-call(s32[1,128]{1,0:T(1,128)S(1)} %copy-done.4, ...), custom_call_target="tpu_custom_call" | custom-call | flops 1610612736 | bytes 16777216 | tf_op jit(solution)/shard_map/qkv/pallas_call | solution.py:249
  90.9 1.9 %collective-permute-start.3 = (bf16[128,384]{1,0:T(8,128)(2,1)S(1)}, bf16[128,384]{1,0:T(8,128)(2,1)S(1)}, u32[]{:S(2)}, u32[]{:S(2)}) collective-permute-start(bf16[128,384]{1,0:T(8,128)(2,1)S(1)} %get-tuple-element.22), channel_id=1, source_target_pairs={{0,4},{1,5},{2,6},{3,7},{4,0},{5,1},{6,2},{7,3},{8,12},{9,13},{10,... | collective-permute-start | bytes 294920 | tf_op jit(solution)/shard_map/ppermute | solution.py:196
  92.8 2.6 %collective-permute-start.4 = (bf16[128,384]{1,0:T(8,128)(2,1)S(1)}, bf16[128,384]{1,0:T(8,128)(2,1)S(1)}, u32[]{:S(2)}, u32[]{:S(2)}) collective-permute-start(bf16[128,384]{1,0:T(8,128)(2,1)S(1)} %get-tuple-element.23), channel_id=1, source_target_pairs={{0,5},{1,6},{2,7},{3,0},{4,1},{5,2},{6,3},{7,4},{8,13},{9,14},{10,... | collective-permute-start | bytes 294920 | tf_op jit(solution)/shard_map/ppermute | solution.py:196
  95.4 5.3 %collective-permute-done.1.refs_2_ = bf16[128,384]{1,0:T(8,128)(2,1)S(1)} collective-permute-done((bf16[128,384]{1,0:T(8,128)(2,1)S(1)}, bf16[128,384]{1,0:T(8,128)(2,1)S(1)}, u32[]{:S(2)}, u32[]{:S(2)}) %collective-permute-start.1) | collective-permute-done | bytes 98336 | tf_op jit(solution)/shard_map/ppermute | solution.py:196
  101.4 3.8 %collective-permute-done.6.refs_7_ = bf16[128,384]{1,0:T(8,128)(2,1)S(1)} collective-permute-done((bf16[128,384]{1,0:T(8,128)(2,1)S(1)}, bf16[128,384]{1,0:T(8,128)(2,1)S(1)}, u32[]{:S(2)}, u32[]{:S(2)}) %collective-permute-start.6) | collective-permute-done | bytes 98336 | tf_op jit(solution)/shard_map/ppermute | solution.py:196
  105.2 1.9 %attention.1 = (bf16[128,128]{1,0:T(8,128)(2,1)S(1)}, bf16[128,128]{1,0:T(8,128)(2,1)S(1)}, bf16[128,128]{1,0:T(8,128)(2,1)S(1)}, bf16[128,128]{1,0:T(8,128)(2,1...) custom-call(bf16[128,384]{1,0:T(8,128)(2,1)S(1)} %get-tuple-element., ...), custom_call_target="tpu_custom_call" | custom-call | flops 536870912 | bytes 2097152 | tf_op jit(solution)/shard_map/attention/pallas_call | solution.py:264
  107.4 2.2 %collective-permute-start.11 = (bf16[128,128]{1,0:T(8,128)(2,1)S(1)}, bf16[128,128]{1,0:T(8,128)(2,1)S(1)}, u32[]{:S(2)}, u32[]{:S(2)}) collective-permute-start(bf16[128,128]{1,0:T(8,128)(2,1)S(1)} %get-tuple-element.31), channel_id=1, source_target_pairs={{0,5},{1,6},{2,7},{3,0},{4,1},{5,2},{6,3},{7,4},{8,13},{9,14},{10,... | collective-permute-start | bytes 98312 | tf_op jit(solution)/shard_map/ppermute | solution.py:196
  109.5 1.2 collective-permute-start.13
  110.7 1.6 %collective-permute-start.7 = (bf16[128,128]{1,0:T(8,128)(2,1)S(1)}, bf16[128,128]{1,0:T(8,128)(2,1)S(1)}, u32[]{:S(2)}, u32[]{:S(2)}) collective-permute-start(bf16[128,128]{1,0:T(8,128)(2,1)S(1)} %get-tuple-element.27), channel_id=1, source_target_pairs={{0,1},{1,2},{2,3},{3,4},{4,5},{5,6},{6,7},{7,0},{8,9},{9,10},{10,1... | collective-permute-start | bytes 98312 | tf_op jit(solution)/shard_map/ppermute | solution.py:196
  113.4 1.2 collective-permute-done.13.refs_7_
  114.6 1.7 %collective-permute-done.8.refs_2_ = bf16[128,128]{1,0:T(8,128)(2,1)S(1)} collective-permute-done((bf16[128,128]{1,0:T(8,128)(2,1)S(1)}, bf16[128,128]{1,0:T(8,128)(2,1)S(1)}, u32[]{:S(2)}, u32[]{:S(2)}) %collective-permute-start.8) | collective-permute-done | bytes 32800 | tf_op jit(solution)/shard_map/ppermute | solution.py:196
  116.3 1.4 %collective-permute-done.9.refs_3_ = bf16[128,128]{1,0:T(8,128)(2,1)S(1)} collective-permute-done((bf16[128,128]{1,0:T(8,128)(2,1)S(1)}, bf16[128,128]{1,0:T(8,128)(2,1)S(1)}, u32[]{:S(2)}, u32[]{:S(2)}) %collective-permute-start.9) | collective-permute-done | bytes 32800 | tf_op jit(solution)/shard_map/ppermute | solution.py:196
  118.5 7.3 %grad.1 = f32[512,2048]{1,0:T(8,128)} custom-call(s32[128,1,128]{2,1,0:T(1,128)S(1)} %all_to_all.21.ids_ref, bf16[1024,1024]{1,0:T(8,128)(2,1)} %bitcast.6.cot_ref), custom_call_target="tpu_custom_call" | custom-call | flops 2147483648 | bytes 6291456 | tf_op jit(solution)/shard_map/grad/pallas_call | solution.py:233
  (34 shorter events, 6.6 us)
Async XLA Ops:
  7.2 41.9 %all-gather.3.cloned.1.call-start = ((), (), s32[]{:S(2)}) async-start(), calls=%async_computation.3 | async-start | bytes 4718592 | tf_op jit(solution)/shard_map/all_gather | solution.py:214
  29.3 1.6 %copy-start.5 = (bf16[512,2048]{1,0:T(8,128)(2,1)S(1)}, bf16[512,2048]{1,0:T(8,128)(2,1)}, u32[]{:S(2)}) copy-start(bf16[512,2048]{1,0:T(8,128)(2,1)} %table_ref.1) | copy-start | bytes 6291460
  33.6 1.3 copy-start.2
  34.9 35.0 %all-to-all-start.1 = ((bf16[128,8,1024]{2,1,0:T(8,128)(2,1)}), bf16[128,8,1024]{2,1,0:T(8,128)(2,1)S(1)}, u32[]{:S(2)}, u32[]{:S(2)}) async-start(bf16[128,8,1024]{2,1,0:T(8,128)(2,1)} %bitcast.9), calls=%async_computation.1 | async-start | bytes 4194304 | tf_op jit(solution)/shard_map/all_to_all | solution.py:190
  49.0 2.2 %copy-start.1 = (bf16[1,1024,2048]{2,1,0:T(8,128)(2,1)S(1)}, bf16[1,1024,2048]{2,1,0:T(8,128)(2,1)}, u32[]{:S(2)}) copy-start(bf16[1,1024,2048]{2,1,0:T(8,128)(2,1)} %all-gather.3.cloned.1.call-done) | copy-start | bytes 12582916
  53.9 24.5 %copy-start.6 = (bf16[2048]{0:T(1024)(128)(2,1)S(1)}, bf16[2048]{0:T(1024)(128)(2,1)}, u32[]{:S(2)}) copy-start(bf16[2048]{0:T(1024)(128)(2,1)} %param.10) | copy-start | bytes 12292
  53.9 24.5 %copy-start.3 = (bf16[1,128,2048]{2,1,0:T(8,128)(2,1)S(1)}, bf16[1,128,2048]{2,1,0:T(8,128)(2,1)}, u32[]{:S(2)}) copy-start(bf16[1,128,2048]{2,1,0:T(8,128)(2,1)} %param.6) | copy-start | bytes 1572868
  53.9 24.5 %copy-start.4 = (s32[1,128]{1,0:T(1,128)S(1)}, s32[1,128]{1,0:T(1,128)}, u32[]{:S(2)}) copy-start(s32[1,128]{1,0:T(1,128)} %ids_ref.1) | copy-start | bytes 1540
  69.9 48.6 %all-to-all-start.2 = ((bf16[16,64,1024]{2,1,0:T(8,128)(2,1)}), bf16[16,64,1024]{2,1,0:T(8,128)(2,1)}, u32[]{:S(2)}, u32[]{:S(2)}) async-start(bf16[16,64,1024]{2,1,0:T(8,128)(2,1)} %cot_slots.1), calls=%async_computation.2 | async-start | bytes 4194304 | tf_op jit(solution)/shard_map/all_to_all | solution.py:190
  78.4 4.6 %copy-start = (bf16[2048,3072]{1,0:T(8,128)(2,1)S(1)}, bf16[2048,3072]{1,0:T(8,128)(2,1)}, u32[]{:S(2)}) copy-start(bf16[2048,3072]{1,0:T(8,128)(2,1)} %w_hbm.1) | copy-start | bytes 37748740
  88.5 6.9 %collective-permute-start = (bf16[128,384]{1,0:T(8,128)(2,1)S(1)}, bf16[128,384]{1,0:T(8,128)(2,1)S(1)}, u32[]{:S(2)}, u32[]{:S(2)}) collective-permute-start(bf16[128,384]{1,0:T(8,128)(2,1)S(1)} %get-tuple-element.19), channel_id=1, source_target_pairs={{0,1},{1,2},{2,3},{3,4},{4,5},{5,6},{6,7},{7,0},{8,9},{9,10},{10,1... | collective-permute-start | bytes 294920 | tf_op jit(solution)/shard_map/ppermute | solution.py:196
  89.3 11.5 %collective-permute-start.1 = (bf16[128,384]{1,0:T(8,128)(2,1)S(1)}, bf16[128,384]{1,0:T(8,128)(2,1)S(1)}, u32[]{:S(2)}, u32[]{:S(2)}) collective-permute-start(bf16[128,384]{1,0:T(8,128)(2,1)S(1)} %get-tuple-element.20), channel_id=1, source_target_pairs={{0,2},{1,3},{2,4},{3,5},{4,6},{5,7},{6,0},{7,1},{8,10},{9,11},{10,... | collective-permute-start | bytes 294920 | tf_op jit(solution)/shard_map/ppermute | solution.py:196
  90.5 10.9 %collective-permute-start.2 = (bf16[128,384]{1,0:T(8,128)(2,1)S(1)}, bf16[128,384]{1,0:T(8,128)(2,1)S(1)}, u32[]{:S(2)}, u32[]{:S(2)}) collective-permute-start(bf16[128,384]{1,0:T(8,128)(2,1)S(1)} %get-tuple-element.21), channel_id=1, source_target_pairs={{0,3},{1,4},{2,5},{3,6},{4,7},{5,0},{6,1},{7,2},{8,11},{9,12},{10,... | collective-permute-start | bytes 294920 | tf_op jit(solution)/shard_map/ppermute | solution.py:196
  90.9 10.4 %collective-permute-start.3 = (bf16[128,384]{1,0:T(8,128)(2,1)S(1)}, bf16[128,384]{1,0:T(8,128)(2,1)S(1)}, u32[]{:S(2)}, u32[]{:S(2)}) collective-permute-start(bf16[128,384]{1,0:T(8,128)(2,1)S(1)} %get-tuple-element.22), channel_id=1, source_target_pairs={{0,4},{1,5},{2,6},{3,7},{4,0},{5,1},{6,2},{7,3},{8,12},{9,13},{10,... | collective-permute-start | bytes 294920 | tf_op jit(solution)/shard_map/ppermute | solution.py:196
  92.8 8.6 %collective-permute-start.4 = (bf16[128,384]{1,0:T(8,128)(2,1)S(1)}, bf16[128,384]{1,0:T(8,128)(2,1)S(1)}, u32[]{:S(2)}, u32[]{:S(2)}) collective-permute-start(bf16[128,384]{1,0:T(8,128)(2,1)S(1)} %get-tuple-element.23), channel_id=1, source_target_pairs={{0,5},{1,6},{2,7},{3,0},{4,1},{5,2},{6,3},{7,4},{8,13},{9,14},{10,... | collective-permute-start | bytes 294920 | tf_op jit(solution)/shard_map/ppermute | solution.py:196
  95.4 6.0 %collective-permute-start.5 = (bf16[128,384]{1,0:T(8,128)(2,1)S(1)}, bf16[128,384]{1,0:T(8,128)(2,1)S(1)}, u32[]{:S(2)}, u32[]{:S(2)}) collective-permute-start(bf16[128,384]{1,0:T(8,128)(2,1)S(1)} %get-tuple-element.24), channel_id=1, source_target_pairs={{0,6},{1,7},{2,0},{3,1},{4,2},{5,3},{6,4},{7,5},{8,14},{9,15},{10,... | collective-permute-start | bytes 294920 | tf_op jit(solution)/shard_map/ppermute | solution.py:196
  100.8 4.4 %collective-permute-start.6 = (bf16[128,384]{1,0:T(8,128)(2,1)S(1)}, bf16[128,384]{1,0:T(8,128)(2,1)S(1)}, u32[]{:S(2)}, u32[]{:S(2)}) collective-permute-start(bf16[128,384]{1,0:T(8,128)(2,1)S(1)} %get-tuple-element.25), channel_id=1, source_target_pairs={{0,7},{1,0},{2,1},{3,2},{4,3},{5,4},{6,5},{7,6},{8,15},{9,8},{10,9... | collective-permute-start | bytes 294920 | tf_op jit(solution)/shard_map/ppermute | solution.py:196
  107.1 5.3 %collective-permute-start.10 = (bf16[128,128]{1,0:T(8,128)(2,1)S(1)}, bf16[128,128]{1,0:T(8,128)(2,1)S(1)}, u32[]{:S(2)}, u32[]{:S(2)}) collective-permute-start(bf16[128,128]{1,0:T(8,128)(2,1)S(1)} %get-tuple-element.30), channel_id=1, source_target_pairs={{0,4},{1,5},{2,6},{3,7},{4,0},{5,1},{6,2},{7,3},{8,12},{9,13},{10,... | collective-permute-start | bytes 98312 | tf_op jit(solution)/shard_map/ppermute | solution.py:196
  107.4 5.4 %collective-permute-start.11 = (bf16[128,128]{1,0:T(8,128)(2,1)S(1)}, bf16[128,128]{1,0:T(8,128)(2,1)S(1)}, u32[]{:S(2)}, u32[]{:S(2)}) collective-permute-start(bf16[128,128]{1,0:T(8,128)(2,1)S(1)} %get-tuple-element.31), channel_id=1, source_target_pairs={{0,5},{1,6},{2,7},{3,0},{4,1},{5,2},{6,3},{7,4},{8,13},{9,14},{10,... | collective-permute-start | bytes 98312 | tf_op jit(solution)/shard_map/ppermute | solution.py:196
  109.5 3.9 %collective-permute-start.12 = (bf16[128,128]{1,0:T(8,128)(2,1)S(1)}, bf16[128,128]{1,0:T(8,128)(2,1)S(1)}, u32[]{:S(2)}, u32[]{:S(2)}) collective-permute-start(bf16[128,128]{1,0:T(8,128)(2,1)S(1)} %get-tuple-element.32), channel_id=1, source_target_pairs={{0,6},{1,7},{2,0},{3,1},{4,2},{5,3},{6,4},{7,5},{8,14},{9,15},{10,... | collective-permute-start | bytes 98312 | tf_op jit(solution)/shard_map/ppermute | solution.py:196
  109.5 5.0 %collective-permute-start.13 = (bf16[128,128]{1,0:T(8,128)(2,1)S(1)}, bf16[128,128]{1,0:T(8,128)(2,1)S(1)}, u32[]{:S(2)}, u32[]{:S(2)}) collective-permute-start(bf16[128,128]{1,0:T(8,128)(2,1)S(1)} %get-tuple-element.33), channel_id=1, source_target_pairs={{0,7},{1,0},{2,1},{3,2},{4,3},{5,4},{6,5},{7,6},{8,15},{9,8},{10,9... | collective-permute-start | bytes 98312 | tf_op jit(solution)/shard_map/ppermute | solution.py:196
  110.7 3.9 %collective-permute-start.7 = (bf16[128,128]{1,0:T(8,128)(2,1)S(1)}, bf16[128,128]{1,0:T(8,128)(2,1)S(1)}, u32[]{:S(2)}, u32[]{:S(2)}) collective-permute-start(bf16[128,128]{1,0:T(8,128)(2,1)S(1)} %get-tuple-element.27), channel_id=1, source_target_pairs={{0,1},{1,2},{2,3},{3,4},{4,5},{5,6},{6,7},{7,0},{8,9},{9,10},{10,1... | collective-permute-start | bytes 98312 | tf_op jit(solution)/shard_map/ppermute | solution.py:196
  112.3 4.0 %collective-permute-start.8 = (bf16[128,128]{1,0:T(8,128)(2,1)S(1)}, bf16[128,128]{1,0:T(8,128)(2,1)S(1)}, u32[]{:S(2)}, u32[]{:S(2)}) collective-permute-start(bf16[128,128]{1,0:T(8,128)(2,1)S(1)} %get-tuple-element.28), channel_id=1, source_target_pairs={{0,2},{1,3},{2,4},{3,5},{4,6},{5,7},{6,0},{7,1},{8,10},{9,11},{10,... | collective-permute-start | bytes 98312 | tf_op jit(solution)/shard_map/ppermute | solution.py:196
  112.8 5.0 %collective-permute-start.9 = (bf16[128,128]{1,0:T(8,128)(2,1)S(1)}, bf16[128,128]{1,0:T(8,128)(2,1)S(1)}, u32[]{:S(2)}, u32[]{:S(2)}) collective-permute-start(bf16[128,128]{1,0:T(8,128)(2,1)S(1)} %get-tuple-element.29), channel_id=1, source_target_pairs={{0,3},{1,4},{2,5},{3,6},{4,7},{5,0},{6,1},{7,2},{8,11},{9,12},{10,... | collective-permute-start | bytes 98312 | tf_op jit(solution)/shard_map/ppermute | solution.py:196
Sparse Core Ops, SparseCore 0:
  9.7 39.2 all-gather.2

commit v3 on v2

v3 whole, which is shorter than its diff:
```python
import functools

import jax
import jax.numpy as jnp
from jax import lax
from jax.experimental import pallas as pl
from jax.experimental.pallas import tpu as pltpu
from jax.sharding import PartitionSpec as P

HEAD = 128
HEADS = 8
CAP = 4
TILE = 2 * CAP
HALF = 1024
MB = 1024 * 1024
AHEAD = 3
BOTH = ("table", "ctx")


def iota(shape, dim):
    return lax.broadcasted_iota(jnp.int32, shape, dim)


def dot(a, b, dims=(((1,), (0,)), ((), ()))):
    return lax.dot_general(a, b, dims, preferred_element_type=jnp.float32)


def onehot(mask):
    return jnp.where(mask, 1.0, 0.0).astype(jnp.bfloat16)


def owner_grid(ids, held):
    n = ids.shape[1]
    owner = jnp.broadcast_to(ids, (n, n)) // held
    return owner, owner.astype(jnp.float32).T.astype(jnp.int32)


def asked_rows(ids_ref, held):
    n, _, tokens = ids_ref.shape
    me = lax.axis_index("table") * lax.axis_size("ctx") + lax.axis_index("ctx")
    wide = jnp.broadcast_to(ids_ref[...], (n, TILE, tokens)).reshape(n * TILE, tokens)
    local = wide - me * held
    mine = (local >= 0) & (local < held)
    earlier = onehot(iota((tokens, tokens), 0) < iota((tokens, tokens), 1))
    rank = dot(onehot(mine), earlier)
    slot = (iota(wide.shape, 0) % CAP).astype(jnp.float32)
    return jnp.where(mine & (rank == slot), local + 1, 0)


def pack_kernel(held, ids_ref, cot_ref, send_hbm, stage_ref, sem):
    tokens = ids_ref.shape[1]
    own_lane, own_sub = owner_grid(ids_ref[...], held)
    earlier = iota((tokens, tokens), 0) < iota((tokens, tokens), 1)
    rank = jnp.sum(jnp.where((own_lane == own_sub) & earlier, 1, 0), axis=0, keepdims=True)
    slot = own_lane[0:1] * TILE + rank
    at = iota((stage_ref.shape[0] * TILE, tokens), 0)
    made = dot(onehot(at == slot), cot_ref[:, :HALF]) + dot(onehot(at == slot + CAP), cot_ref[:, HALF:])
    stage_ref[...] = made.astype(jnp.bfloat16).reshape(stage_ref.shape)
    copy = pltpu.make_async_copy(stage_ref, send_hbm.at[:, 1], sem)
    copy.start()
    copy.wait()


def rows_kernel(ids_ref, table_ref, cot_hbm, send_hbm, stage_ref, sems):
    held = table_ref.shape[0]
    asked = asked_rows(ids_ref, held)
    row = jnp.sum(asked.astype(jnp.float32), axis=1, keepdims=True).astype(jnp.int32)
    parts = sems.shape[0]
    block = row.shape[0] // parts
    shape = (block, held)
    upper = iota(shape, 0) % TILE >= CAP
    copies = []
    for part in range(parts):
        hit = row[part * block : (part + 1) * block] == iota(shape, 1) + 1
        made = dot(onehot(hit & ~upper), table_ref[:, :HALF]) + dot(
            onehot(hit & upper), table_ref[:, HALF:]
        )
        at = pl.ds(part * (block // TILE), block // TILE)
        stage_ref[at] = made.astype(jnp.bfloat16).reshape(block // TILE, TILE, HALF)
        copies.append(
            pltpu.make_async_copy(stage_ref.at[at], send_hbm.at[at, 0], sems.at[part])
        )
        copies[-1].start()
    for copy in copies:
        copy.wait()


def prepare_kernel(ids_ref, gain_ref, low_ref, high_ref, wide_gain_ref):
    wide_gain_ref[...] = jnp.broadcast_to(gain_ref[...].astype(jnp.float32), wide_gain_ref.shape)
    asked = asked_rows(ids_ref, low_ref.shape[0])
    lanes = (((1,), (1,)), ((), ()))
    ones = jnp.ones((8, asked.shape[1]), jnp.bfloat16)
    top = asked // 256
    row = 256.0 * dot(ones, top.astype(jnp.float32).astype(jnp.bfloat16), lanes) + dot(
        ones, (asked - top * 256).astype(jnp.float32).astype(jnp.bfloat16), lanes
    )
    shape = low_ref.shape
    hit = row[0:1].astype(jnp.int32) == iota(shape, 0) + 1
    upper = iota(shape, 1) % TILE >= CAP
    low_ref[...] = onehot(hit & ~upper)
    high_ref[...] = onehot(hit & upper)


def grad_kernel(low_ref, high_ref, cot_ref, grad_ref):
    step = pl.program_id(0)
    cot = cot_ref[...].reshape(low_ref.shape[1], grad_ref.shape[1])

    @pl.when(step % 2 == 0)
    def _():
        grad_ref[...] = dot(low_ref[...], cot)

    @pl.when(step % 2 == 1)
    def _():
        grad_ref[...] = dot(high_ref[...], cot)


def qkv_kernel(
    held, ids_ref, got_hbm, base_ref, gain_ref, w_hbm, low_hbm, high_hbm, out_ref, got_ref, w_ref,
    normed_ref, sems,
):
    blocks, _, per = w_ref.shape
    load = pltpu.make_async_copy(got_hbm.at[:, 0], got_ref, sems.at[blocks])
    load.start()
    copies = [
        pltpu.make_async_copy(w_hbm.at[:, j * per : (j + 1) * per], w_ref.at[j], sems.at[j])
        for j in range(blocks)
    ]
    for copy in copies[:AHEAD]:
        copy.start()
    n = ids_ref.shape[1]
    slots = got_ref.shape[0] * TILE
    own_lane, own_sub = owner_grid(ids_ref[...], held)
    same = (own_lane == own_sub) & (iota((n, n), 1) < iota((n, n), 0))
    rank = jnp.sum(jnp.where(same, 1, 0), axis=1, keepdims=True)
    slot = own_sub[:, 0:1] * TILE + rank
    pick = onehot(iota((2 * n, slots), 1) == jnp.concatenate([slot, slot + CAP], axis=0))
    load.wait()
    rows = dot(pick, got_ref[...].reshape(slots, HALF))
    low = base_ref[:, :HALF].astype(jnp.float32) + rows[:n]
    high = base_ref[:, HALF:].astype(jnp.float32) + rows[n:]
    square = jnp.sum(low * low, axis=1, keepdims=True) + jnp.sum(high * high, axis=1, keepdims=True)
    scale = lax.rsqrt(square * (1.0 / (2 * HALF)) + 1e-05)
    gain = gain_ref[0:1]
    normed_ref[:, :HALF] = (low * scale * gain[:, :HALF]).astype(jnp.bfloat16)
    normed_ref[:, HALF:] = (high * scale * gain[:, HALF:]).astype(jnp.bfloat16)
    for j, copy in enumerate(copies):
        copy.wait()
        if j + AHEAD < blocks:
            copies[j + AHEAD].start()
        made = dot(normed_ref[...], w_ref[j]).astype(jnp.bfloat16)
        for i in range(per // HEAD):
            kind, head = divmod(j * per // HEAD + i, HEADS)
            out_ref[head, :, kind * HEAD : (kind + 1) * HEAD] = made[:, i * HEAD : (i + 1) * HEAD]


def spread_kernel(ids_ref, out_ref):
    out_ref[...] = jnp.broadcast_to(ids_ref[...][None], out_ref.shape)


def attention_kernel(block, qkv_ref, out_ref):
    seq = qkv_ref.shape[0]
    for i in range(seq // block):
        count = (i + 1) * block
        query = qkv_ref[i * block : count, :HEAD]
        keys = qkv_ref[:count, HEAD : 2 * HEAD]
        values = qkv_ref[:count, 2 * HEAD :]
        scores = dot(query, keys, (((1,), (1,)), ((), ()))) * HEAD ** (-0.5)
        allowed = iota((block, count), 1) <= iota((block, count), 0) + i * block
        scores = jnp.where(allowed, scores, -1e30)
        top = jnp.max(scores, axis=1, keepdims=True)
        weights = jnp.where(allowed, jnp.exp(scores - top), 0.0)
        total = jnp.sum(weights, axis=1, keepdims=True)
        mixed = dot(weights.astype(jnp.bfloat16), values)
        out_ref[i * block : count, :] = (mixed / total).astype(jnp.bfloat16)


def call(kernel, out, flops, moved, mb=24, **kwargs):
    return pl.pallas_call(
        kernel,
        out_shape=out,
        compiler_params=pltpu.CompilerParams(vmem_limit_bytes=mb * MB),
        cost_estimate=pl.CostEstimate(flops=flops, bytes_accessed=moved, transcendentals=0),
        **kwargs,
    )


def exchange(x, axes):
    return lax.all_to_all(x, axes, split_axis=0, concat_axis=0, tiled=True)


def shards(base_embed, ngram_ids, ngram_table, embed_cot, norm_gain, w_qkv):
    tokens = ngram_ids.shape[1]
    width = base_embed.shape[2]
    held = ngram_table.shape[0]
    table = lax.axis_size("table")
    ctx = lax.axis_size("ctx")
    owners = table * ctx
    slots = owners * TILE
    columns = w_qkv.shape[1]
    bf16, f32 = jnp.bfloat16, jnp.float32
    shape = jax.ShapeDtypeStruct
    whole = pl.BlockSpec(memory_space=pltpu.VMEM)
    remote = pl.BlockSpec(memory_space=pltpu.HBM)

    near_hbm = pltpu.with_memory_space_constraint(ngram_ids, pltpu.HBM)
    all_ids = exchange(
        call(spread_kernel, shape((owners, 1, tokens), jnp.int32), 0, 0, name="spread")(near_hbm), BOTH
    )
    blocks = pltpu.HBM((owners, 2, TILE, HALF), bf16)
    stage = pltpu.VMEM((owners, TILE, HALF), bf16)
    send = call(
        functools.partial(pack_kernel, held),
        blocks,
        2 * slots * tokens * width,
        3 * MB,
        name="pack",
        in_specs=[whole] * 2,
        out_specs=remote,
        scratch_shapes=[stage, pltpu.SemaphoreType.DMA],
    )(ngram_ids, embed_cot[0])
    send = call(
        rows_kernel,
        blocks,
        2 * slots * held * width,
        4 * MB,
        name="rows",
        in_specs=[whole, whole, remote],
        out_specs=remote,
        scratch_shapes=[stage, pltpu.SemaphoreType.DMA((4,))],
        input_output_aliases={2: 0},
    )(all_ids, ngram_table, send)
    got = exchange(send, BOTH)
    low, high, gain = call(
        prepare_kernel,
        [pltpu.VMEM((held, slots), bf16)] * 2 + [shape((8, width), f32)],
        20000 * MB,
        2 * MB,
        name="prepare",
    )(all_ids, norm_gain.reshape(1, width))
    w_blocks = 8
    qkv = call(
        functools.partial(qkv_kernel, held),
        shape((ctx, tokens, 3 * HEAD), bf16),
        2 * tokens * width * columns,
        16 * MB,
        name="qkv",
        in_specs=[whole, remote, whole, whole, remote, remote, remote],
        out_specs=whole,
        scratch_shapes=[
            stage,
            pltpu.VMEM((w_blocks, width, columns // w_blocks), bf16),
            pltpu.VMEM((tokens, width), bf16),
            pltpu.SemaphoreType.DMA((w_blocks + 1,)),
        ],
    )(
        ngram_ids,
        got,
        base_embed[0],
        gain,
        pltpu.with_memory_space_constraint(w_qkv, pltpu.HBM),
        low,
        high,
    )
    steps = 4
    per = width // steps
    table_grad = call(
        grad_kernel,
        shape((held, width), f32),
        2 * slots * held * width,
        6 * MB,
        name="grad",
        grid=(steps,),
        in_specs=[
            pl.BlockSpec((held, slots), lambda j: (0, 0)),
            pl.BlockSpec((held, slots), lambda j: (0, 0)),
            pl.BlockSpec((owners, None, TILE, per), lambda j: (0, 1, 0, j // 2)),
        ],
        out_specs=pl.BlockSpec((held, per), lambda j: (0, j % 2 * 2 + j // 2)),
    )(low, high, got)
    mine = exchange(qkv, "ctx").reshape(ctx * tokens, 3 * HEAD)
    mixed = call(
        functools.partial(attention_kernel, 256),
        shape((ctx * tokens, HEAD), bf16),
        4 * ctx * tokens * ctx * tokens * HEAD,
        2 * MB,
        name="attention",
    )(mine)
    context = exchange(mixed.reshape(ctx, tokens, HEAD), "ctx")
    context = context.transpose(1, 0, 2).reshape(tokens, HEADS * HEAD)
    return (context[None], table_grad)


def solution(mesh):
    return jax.shard_map(
        shards,
        mesh=mesh,
        in_specs=(
            P("table", "ctx", None),
            P("table", "ctx"),
            P(("table", "ctx"), None),
            P("table", "ctx", None),
            P(),
            P(),
        ),
        out_specs=(P("table", "ctx", None), P(("table", "ctx"), None)),
        check_vma=False,
    )
```

time: 133 us -> 122 us (0.917)
  waiting for transfers between devices: 40.3 us -> 56.7 us
  between operations: 14.1 us -> 0.74 us
  local copies, waits for them, and re-layouts: 10.4 us -> 2.71 us
  blocking collectives: 20.7 us -> 15.7 us
  starting transfers between devices: 26.3 us -> 21.6 us
  Pallas kernels: 20.9 us -> 24.1 us
    all_to_all x2 -> x3, waiting for transfers between devices: 16 us -> 56.7 us  [exchange(): return lax.all_to_all(x, axes, split_axis=0, concat_axis=0, tiled=True)]
    ppermute x14 -> x0, waiting for transfers between devices: 14.1 us -> none  [shift_all(): lax.ppermute(pieces[k], 'ctx', [(i, (i + k) % n) for i in range(n)])]
    ppermute x14 -> x0, starting transfers between devices: 13.2 us -> none  [shift_all(): lax.ppermute(pieces[k], 'ctx', [(i, (i + k) % n) for i in range(n)])]
    all_gather x1 -> x0, waiting for transfers between devices: 9.5 us -> none  [shards(): seq_cot = lax.all_gather(embed_cot[0], 'ctx', axis=0, tiled=True)]
    all_to_all x2 -> x3, starting transfers between devices: 13 us -> 21.6 us  [exchange(): return lax.all_to_all(x, axes, split_axis=0, concat_axis=0, tiled=True)]
    unnamed x14 -> x12, local copies, waits for them, and re-layouts: 9.69 us -> 1.71 us
    all_to_all x1, blocking collectives: 20.7 us -> 15.7 us  [exchange(): return lax.all_to_all(x, axes, split_axis=0, concat_axis=0, tiled=True)]
    pallas_call x5 -> x6, Pallas kernels: 13.5 us -> 17.9 us  [the longest x1 6.59 us: shards(): call(functools.partial(qkv_kernel, held), shape((ctx, tokens, 3 * HEAD),...]
  transfers between devices with their start and end apart: 17 -> 3, of which waited for: 8 -> 3; matrix products, arithmetic and copies ran while one was open for 1% -> 0% of each run, Pallas kernels for 10% -> 8%
where the time goes in v3:
time: 122 us; the launch traced here: 121 us
  waiting for transfers between devices  56.7 us (46%)
  Pallas kernels  24.1 us (20%)
  starting transfers between devices  21.6 us (18%)
  blocking collectives  15.7 us (13%)
  local copies, waits for them, and re-layouts  2.71 us (2%)
    all_to_all x3, waiting for transfers between devices, exchange(): return lax.all_to_all(x, axes, split_axis=0, concat_axis=0, tiled=True)  56.7 us
    all_to_all x3, starting transfers between devices, exchange(): return lax.all_to_all(x, axes, split_axis=0, concat_axis=0, tiled=True)  21.6 us
    all_to_all x1, blocking collectives, exchange(): return lax.all_to_all(x, axes, split_axis=0, concat_axis=0, tiled=True)  15.7 us
    pallas_call x1, Pallas kernels, shards(): call(functools.partial(qkv_kernel, held), shape((ctx, tokens, 3 * HEAD),...  6.59 us
    pallas_call x1, Pallas kernels, shards(): call(grad_kernel, shape((held, width), f32), 2 * slots * held * width, 6...  6.17 us
    pallas_call x1, Pallas kernels, shards(): call(rows_kernel, blocks, 2 * slots * held * width, 4 * MB, name='rows',...  3.42 us
    pallas_call x1, Pallas kernels, shards(): call(functools.partial(pack_kernel, held), blocks, 2 * slots * tokens * w...  2.68 us
    pallas_call x1, Pallas kernels, shards(): call(functools.partial(attention_kernel, 256), shape((ctx * tokens, HEAD)...  2.47 us
  transfers between devices with their start and end apart: 3, of which 3 were waited for; matrix products, arithmetic and copies ran while one was open for 0% of the time, Pallas kernels for 8%

profile of v3, /device:TPU:1, one launch (start us, length us, event | category | flops | bytes accessed | tf_op | source)
XLA Modules:
  0.0 121.5 jit_solution(16974727818337685998)
XLA Ops:
  0.6 1.5 %spread.1 = s32[128,1,128]{2,1,0:T(1,128)} custom-call(s32[1,128]{1,0:T(1,128)} %ids_ref.5), custom_call_target="tpu_custom_call" | custom-call | tf_op jit(solution)/shard_map/spread/pallas_call | solution.py:207
  2.1 11.5 %all-to-all-start = ((s32[128,1,128]{2,1,0:T(1,128)}), s32[128,1,128]{2,1,0:T(1,128)S(1)}, u32[]{:S(2)}, u32[]{:S(2)}) async-start(s32[128,1,128]{2,1,0:T(1,128)} %spread.1), calls=%async_computation | async-start | bytes 131072 | tf_op jit(solution)/shard_map/all_to_all | solution.py:188
  13.6 0.0 copy-start.1
  13.6 1.0 copy-done.1
  14.7 0.7 copy-done.3
  15.3 2.7 %pack.1.cot_hbm = bf16[128,2,8,1024]{3,2,1,0:T(8,128)(2,1)} custom-call(s32[1,128]{1,0:T(1,128)S(1)} %copy-done.3, bf16[128,2048]{1,0:T(8,128)(2,1)S(1)} %bitcast.6), custom_call_target="tpu_custom_call" | custom-call | flops 536870912 | bytes 3145728 | tf_op jit(solution)/shard_map/pack/pallas_call | solution.py:211
  18.0 4.9 %all-to-all-done.ids_ref = s32[128,1,128]{2,1,0:T(1,128)S(1)} async-done(((s32[128,1,128]{2,1,0:T(1,128)}), s32[128,1,128]{2,1,0:T(1,128)S(1)}, u32[]{:S(2)}, u32[]{:S(2)}) %all-to-all-start) | async-done | bytes 65568 | tf_op jit(solution)/shard_map/all_to_all | solution.py:188
  22.9 3.4 %rows.1 = bf16[128,2,8,1024]{3,2,1,0:T(8,128)(2,1)} custom-call(s32[128,1,128]{2,1,0:T(1,128)S(1)} %all-to-all-done.ids_ref, bf16[512,2048]{1,0:T(8,128)(2,1)S(1)} %copy-done, bf16[128,2,8,1024]{3,2,1,0:T(8,128)(2,1)} %pack.1.cot_hbm), custom_call_target="tpu_custom_call", output_to_operand_aliasing={{}: (2, {})} | custom-call | flops 2147483648 | bytes 4194304 | tf_op jit(solution)/shard_map/rows/pallas_call | solution.py:221
  26.4 0.0 copy-start.5
  26.4 5.7 %all-to-all-start.1 = ((bf16[128,2,8,1024]{3,2,1,0:T(8,128)(2,1)}), bf16[128,2,8,1024]{3,2,1,0:T(8,128)(2,1)}, u32[]{:S(2)}, u32[]{:S(2)}) async-start(bf16[128,2,8,1024]{3,2,1,0:T(8,128)(2,1)} %rows.1), calls=%async_computation.1 | async-start | bytes 8388608 | tf_op jit(solution)/shard_map/all_to_all | solution.py:188
  32.1 0.0 copy-done.5
  32.2 0.0 copy-start.2
  32.2 0.0 copy-start.4
  32.2 1.3 %prepare.1 = (bf16[512,1024]{1,0:T(8,128)(2,1)S(1)}, bf16[512,1024]{1,0:T(8,128)(2,1)S(1)}, f32[8,2048]{1,0:T(8,128)S(1)}) custom-call(s32[128,1,128]{2,1,0:T(1,128)S(1)} %all-to-all-done.ids_ref, bf16[1,2048]{1,0:T(2,128)(2,1)S(1)} %reshape.13.gain_ref), custom_call_target="tpu_custom_call" | custom-call | flops 20971520000 | bytes 2097152 | tf_op jit(solution)/shard_map/prepare/pallas_call | solution.py:233
  33.5 51.4 %all-to-all-done.1.got_hbm.cot_ref = bf16[128,2,8,1024]{3,2,1,0:T(8,128)(2,1)} async-done(((bf16[128,2,8,1024]{3,2,1,0:T(8,128)(2,1)}), bf16[128,2,8,1024]{3,2,1,0:T(8,128)(2,1)}, u32[]{:S(2)}, u32[]{:S(2)}) %all-to-all-start.1) | async-done | bytes 4194336 | tf_op jit(solution)/shard_map/all_to_all | solution.py:188
  84.9 0.0 copy-done.2
  84.9 6.6 %qkv.1 = bf16[8,128,384]{2,1,0:T(8,128)(2,1)S(1)} custom-call(s32[1,128]{1,0:T(1,128)S(1)} %copy-done.4, bf16[128,2,8,1024]{3,2,1,0:T(8,128)(2,1)} %all-to-all-done.1.got_hbm.cot_ref, bf16[128,2048]{1,0:T(8,128)(2,1)S(1)} %bitcast.7, f32[8,2048]{1,0:T(8,128)S(1)} %get-tuple-element.5.gain_ref, bf16[2048,3072]{1,0:T(8,128)(2,1)} %w_hbm.1, ...), custom_call_target="tpu_custom_call" | custom-call | flops 1610612736 | bytes 16777216 | tf_op jit(solution)/shard_map/qkv/pallas_call | solution.py:241
  91.5 15.7 %all_to_all.20 = bf16[8,128,384]{2,1,0:T(8,128)(2,1)S(1)} all-to-all(bf16[8,128,384]{2,1,0:T(8,128)(2,1)S(1)} %qkv.1), channel_id=1, replica_groups=mesh['table'=16,'ctx'=8] {'ctx'}, dimensions={0} | all-to-all | bytes 1572864 | tf_op jit(solution)/shard_map/all_to_all | solution.py:188
  107.2 2.5 %attention.1 = bf16[1024,128]{1,0:T(8,128)(2,1)} custom-call(bf16[1024,384]{1,0:T(8,128)(2,1)S(1)} %bitcast.5), custom_call_target="tpu_custom_call" | custom-call | flops 536870912 | bytes 2097152 | tf_op jit(solution)/shard_map/attention/pallas_call | solution.py:281
  109.6 4.3 %all-to-all-start.3 = ((bf16[8,128,128]{2,1,0:T(8,128)(2,1)}), bf16[8,128,128]{2,1,0:T(8,128)(2,1)S(1)}, u32[]{:S(2)}, u32[]{:S(2)}) async-start(bf16[8,128,128]{2,1,0:T(8,128)(2,1)} %bitcast.3), calls=%async_computation.3 | async-start | bytes 524288 | tf_op jit(solution)/shard_map/all_to_all | solution.py:188
  114.0 6.2 %grad.1 = f32[512,2048]{1,0:T(8,128)} custom-call(bf16[512,1024]{1,0:T(8,128)(2,1)S(1)} %get-tuple-element.6.low_hbm.low_ref, bf16[512,1024]{1,0:T(8,128)(2,1)S(1)} %get-tuple-element.7.high_hbm.high_ref, bf16[128,2,8,1024]{3,2,1,0:T(8,128)(2,1)} %all-to-all-done.1.got_hbm.cot_ref), custom_call_target="tpu_custom_call" | custom-call | flops 2147483648 | bytes 6291456 | tf_op jit(solution)/shard_map/grad/pallas_call | solution.py:266
  120.1 0.4 all-to-all-done.3
  120.5 0.2 copy.9
  120.7 0.8 broadcast_in_dim_reshape.3
  (5 shorter events, 0.0 us)
Async XLA Ops:
  0.6 22.3 %copy-start = (bf16[512,2048]{1,0:T(8,128)(2,1)S(1)}, bf16[512,2048]{1,0:T(8,128)(2,1)}, u32[]{:S(2)}) copy-start(bf16[512,2048]{1,0:T(8,128)(2,1)} %table_ref.1) | copy-start | bytes 6291460
  2.1 20.8 %all-to-all-start = ((s32[128,1,128]{2,1,0:T(1,128)}), s32[128,1,128]{2,1,0:T(1,128)S(1)}, u32[]{:S(2)}, u32[]{:S(2)}) async-start(s32[128,1,128]{2,1,0:T(1,128)} %spread.1), calls=%async_computation | async-start | bytes 131072 | tf_op jit(solution)/shard_map/all_to_all | solution.py:188
  13.6 1.0 copy-start.1
  14.7 0.7 copy-start.3
  26.4 5.8 %copy-start.5 = (bf16[2048]{0:T(1024)(128)(2,1)S(1)}, bf16[2048]{0:T(1024)(128)(2,1)}, u32[]{:S(2)}) copy-start(bf16[2048]{0:T(1024)(128)(2,1)} %param.10) | copy-start | bytes 12292
  26.4 58.5 %all-to-all-start.1 = ((bf16[128,2,8,1024]{3,2,1,0:T(8,128)(2,1)}), bf16[128,2,8,1024]{3,2,1,0:T(8,128)(2,1)}, u32[]{:S(2)}, u32[]{:S(2)}) async-start(bf16[128,2,8,1024]{3,2,1,0:T(8,128)(2,1)} %rows.1), calls=%async_computation.1 | async-start | bytes 8388608 | tf_op jit(solution)/shard_map/all_to_all | solution.py:188
  32.2 52.7 %copy-start.2 = (bf16[1,128,2048]{2,1,0:T(8,128)(2,1)S(1)}, bf16[1,128,2048]{2,1,0:T(8,128)(2,1)}, u32[]{:S(2)}) copy-start(bf16[1,128,2048]{2,1,0:T(8,128)(2,1)} %param.6) | copy-start | bytes 1572868
  32.2 52.7 %copy-start.4 = (s32[1,128]{1,0:T(1,128)S(1)}, s32[1,128]{1,0:T(1,128)}, u32[]{:S(2)}) copy-start(s32[1,128]{1,0:T(1,128)} %ids_ref.5) | copy-start | bytes 1540
  109.6 10.9 %all-to-all-start.3 = ((bf16[8,128,128]{2,1,0:T(8,128)(2,1)}), bf16[8,128,128]{2,1,0:T(8,128)(2,1)S(1)}, u32[]{:S(2)}, u32[]{:S(2)}) async-start(bf16[8,128,128]{2,1,0:T(8,128)(2,1)} %bitcast.3), calls=%async_computation.3 | async-start | bytes 524288 | tf_op jit(solution)/shard_map/all_to_all | solution.py:188

commit v4 on v3

--- a/solution.py
+++ b/solution.py
@@ -13,7 +13,7 @@
 TILE = 2 * CAP
 HALF = 1024
 MB = 1024 * 1024
-AHEAD = 3
+AHEAD = 4
 BOTH = ("table", "ctx")
 
 
@@ -115,14 +115,15 @@
 
 
 def qkv_kernel(
-    held, ids_ref, got_hbm, base_ref, gain_ref, w_hbm, low_hbm, high_hbm, out_ref, got_ref, w_ref,
-    normed_ref, sems,
+    held, ids_ref, got_hbm, base_ref, gain_ref, w_hbm, low_hbm, high_hbm, *refs
 ):
-    blocks, _, per = w_ref.shape
+    *out_refs, got_ref, w_ref, normed_ref, total_ref, made_ref, sems = refs
+    blocks, depth, columns = w_ref.shape
+    per = columns // 6
     load = pltpu.make_async_copy(got_hbm.at[:, 0], got_ref, sems.at[blocks])
     load.start()
     copies = [
-        pltpu.make_async_copy(w_hbm.at[:, j * per : (j + 1) * per], w_ref.at[j], sems.at[j])
+        pltpu.make_async_copy(w_hbm.at[j * depth : (j + 1) * depth], w_ref.at[j], sems.at[j])
         for j in range(blocks)
     ]
     for copy in copies[:AHEAD]:
@@ -147,31 +148,55 @@
         copy.wait()
         if j + AHEAD < blocks:
             copies[j + AHEAD].start()
-        made = dot(normed_ref[...], w_ref[j]).astype(jnp.bfloat16)
-        for i in range(per // HEAD):
-            kind, head = divmod(j * per // HEAD + i, HEADS)
-            out_ref[head, :, kind * HEAD : (kind + 1) * HEAD] = made[:, i * HEAD : (i + 1) * HEAD]
+        part = normed_ref[:, j * depth : (j + 1) * depth]
+        for first in range(0, columns, per):
+            at = slice(first, first + per)
+            made = dot(part, w_ref[j, :, at])
+            if j > 0:
+                made += total_ref[:, at]
+            if j < blocks - 1:
+                total_ref[:, at] = made
+                continue
+            made = made.astype(jnp.bfloat16)
+            for i in range(per // HEAD):
+                kind, head = divmod(first // HEAD + i, HEADS)
+                made_ref[head, :, kind * HEAD : (kind + 1) * HEAD] = made[:, i * HEAD : (i + 1) * HEAD]
+    me = lax.axis_index("ctx")
+    for shift, ref in enumerate(out_refs):
+        ref[...] = made_ref[(me + shift) % HEADS]
 
 
 def spread_kernel(ids_ref, out_ref):
     out_ref[...] = jnp.broadcast_to(ids_ref[...][None], out_ref.shape)
 
 
-def attention_kernel(block, qkv_ref, out_ref):
-    seq = qkv_ref.shape[0]
+def attention_kernel(block, *refs):
+    *ins, mixed_ref, qkv_ref = refs
+    tokens = ins[0].shape[0]
+    seq = tokens * HEADS
+    me = lax.axis_index("ctx")
+    for shift, ref in enumerate(ins):
+        source = (me + HEADS - shift) % HEADS
+        qkv_ref[pl.ds(pl.multiple_of(source * tokens, tokens), tokens), :] = ref[...]
+    lanes = (((1,), (1,)), ((), ()))
+    allowed = iota((block, block), 1) <= iota((block, block), 0)
     for i in range(seq // block):
-        count = (i + 1) * block
-        query = qkv_ref[i * block : count, :HEAD]
-        keys = qkv_ref[:count, HEAD : 2 * HEAD]
-        values = qkv_ref[:count, 2 * HEAD :]
-        scores = dot(query, keys, (((1,), (1,)), ((), ()))) * HEAD ** (-0.5)
-        allowed = iota((block, count), 1) <= iota((block, count), 0) + i * block
+        here = slice(i * block, (i + 1) * block)
+        query = qkv_ref[here, :HEAD]
+        scores = dot(query, qkv_ref[here, HEAD : 2 * HEAD], lanes) * HEAD ** (-0.5)
         scores = jnp.where(allowed, scores, -1e30)
         top = jnp.max(scores, axis=1, keepdims=True)
+        if i > 0:
+            before = dot(query, qkv_ref[: i * block, HEAD : 2 * HEAD], lanes) * HEAD ** (-0.5)
+            top = jnp.maximum(top, jnp.max(before, axis=1, keepdims=True))
         weights = jnp.where(allowed, jnp.exp(scores - top), 0.0)
         total = jnp.sum(weights, axis=1, keepdims=True)
-        mixed = dot(weights.astype(jnp.bfloat16), values)
-        out_ref[i * block : count, :] = (mixed / total).astype(jnp.bfloat16)
+        mixed = dot(weights.astype(jnp.bfloat16), qkv_ref[here, 2 * HEAD :])
+        if i > 0:
+            weights = jnp.exp(before - top)
+            total += jnp.sum(weights, axis=1, keepdims=True)
+            mixed += dot(weights.astype(jnp.bfloat16), qkv_ref[: i * block, 2 * HEAD :])
+        mixed_ref[here, :] = (mixed / total).astype(jnp.bfloat16)
 
 
 def call(kernel, out, flops, moved, mb=24, **kwargs):
@@ -186,6 +211,14 @@
 
 def exchange(x, axes):
     return lax.all_to_all(x, axes, split_axis=0, concat_axis=0, tiled=True)
+
+
+def shift_all(pieces):
+    n = len(pieces)
+    moved = [
+        lax.ppermute(pieces[k], "ctx", [(i, (i + k) % n) for i in range(n)]) for k in range(1, n)
+    ]
+    return [pieces[0], *moved]
 
 
 def shards(base_embed, ngram_ids, ngram_table, embed_cot, norm_gain, w_qkv):
@@ -240,16 +273,18 @@
     w_blocks = 8
     qkv = call(
         functools.partial(qkv_kernel, held),
-        shape((ctx, tokens, 3 * HEAD), bf16),
+        [shape((tokens, 3 * HEAD), bf16)] * HEADS,
         2 * tokens * width * columns,
         16 * MB,
         name="qkv",
         in_specs=[whole, remote, whole, whole, remote, remote, remote],
-        out_specs=whole,
+        out_specs=[whole] * HEADS,
         scratch_shapes=[
             stage,
-            pltpu.VMEM((w_blocks, width, columns // w_blocks), bf16),
+            pltpu.VMEM((w_blocks, width // w_blocks, columns), bf16),
             pltpu.VMEM((tokens, width), bf16),
+            pltpu.VMEM((tokens, columns), f32),
+            pltpu.VMEM((HEADS, tokens, 3 * HEAD), bf16),
             pltpu.SemaphoreType.DMA((w_blocks + 1,)),
         ],
     )(
@@ -277,14 +312,14 @@
         ],
         out_specs=pl.BlockSpec((held, per), lambda j: (0, j % 2 * 2 + j // 2)),
     )(low, high, got)
-    mine = exchange(qkv, "ctx").reshape(ctx * tokens, 3 * HEAD)
     mixed = call(
         functools.partial(attention_kernel, 256),
         shape((ctx * tokens, HEAD), bf16),
         4 * ctx * tokens * ctx * tokens * HEAD,
         2 * MB,
         name="attention",
-    )(mine)
+        scratch_shapes=[pltpu.VMEM((ctx * tokens, 3 * HEAD), bf16)],
+    )(*shift_all(qkv))
     context = exchange(mixed.reshape(ctx, tokens, HEAD), "ctx")
     context = context.transpose(1, 0, 2).reshape(tokens, HEADS * HEAD)
     return (context[None], table_grad)

time: 122 us -> 121 us (level)
  blocking collectives: 15.7 us -> 0 us
  waiting for transfers between devices: 56.7 us -> 65.3 us
  starting transfers between devices: 21.6 us -> 28 us
    all_to_all x1 -> x0, blocking collectives: 15.7 us -> none  [exchange(): return lax.all_to_all(x, axes, split_axis=0, concat_axis=0, tiled=True)]
    ppermute x0 -> x7, waiting for transfers between devices: none -> 8.98 us  [shift_all(): lax.ppermute(pieces[k], 'ctx', [(i, (i + k) % n) for i in range(n)])]
    ppermute x0 -> x7, starting transfers between devices: none -> 7.43 us  [shift_all(): lax.ppermute(pieces[k], 'ctx', [(i, (i + k) % n) for i in range(n)])]
  transfers between devices with their start and end apart: 3 -> 10, of which waited for: 3 -> 5; matrix products, arithmetic and copies ran while one was open for 0% -> 0% of each run, Pallas kernels for 8% -> 8%
where the time goes in v4:
time: 121 us; the launch traced here: 120 us
  waiting for transfers between devices  65.3 us (54%)
  starting transfers between devices  28 us (23%)
  Pallas kernels  23.5 us (19%)
  local copies, waits for them, and re-layouts  2.71 us (2%)
    all_to_all x3, waiting for transfers between devices, exchange(): return lax.all_to_all(x, axes, split_axis=0, concat_axis=0, tiled=True)  56.3 us
    all_to_all x3, starting transfers between devices, exchange(): return lax.all_to_all(x, axes, split_axis=0, concat_axis=0, tiled=True)  20.6 us
    ppermute x7, waiting for transfers between devices, shift_all(): lax.ppermute(pieces[k], 'ctx', [(i, (i + k) % n) for i in range(n)])  8.98 us
    ppermute x7, starting transfers between devices, shift_all(): lax.ppermute(pieces[k], 'ctx', [(i, (i + k) % n) for i in range(n)])  7.43 us
    pallas_call x1, Pallas kernels, shards(): call(grad_kernel, shape((held, width), f32), 2 * slots * held * width, 6...  6.19 us
    pallas_call x1, Pallas kernels, shards(): call(functools.partial(qkv_kernel, held), [shape((tokens, 3 * HEAD), bf16...  5.96 us
    pallas_call x1, Pallas kernels, shards(): call(rows_kernel, blocks, 2 * slots * held * width, 4 * MB, name='rows',...  3.41 us
    pallas_call x1, Pallas kernels, shards(): call(functools.partial(pack_kernel, held), blocks, 2 * slots * tokens * w...  2.68 us
  transfers between devices with their start and end apart: 10, of which 5 were waited for; matrix products, arithmetic and copies ran while one was open for 0% of the time, Pallas kernels for 8%

profile of v4, /device:TPU:1, one launch (start us, length us, event | category | flops | bytes accessed | tf_op | source)
XLA Modules:
  0.0 120.4 jit_solution(17481914705410793056)
XLA Ops:
  0.6 1.5 %spread.1 = s32[128,1,128]{2,1,0:T(1,128)} custom-call(s32[1,128]{1,0:T(1,128)} %ids_ref.5), custom_call_target="tpu_custom_call" | custom-call | tf_op jit(solution)/shard_map/spread/pallas_call | solution.py:240
  2.1 11.5 %all-to-all-start = ((s32[128,1,128]{2,1,0:T(1,128)}), s32[128,1,128]{2,1,0:T(1,128)S(1)}, u32[]{:S(2)}, u32[]{:S(2)}) async-start(s32[128,1,128]{2,1,0:T(1,128)} %spread.1), calls=%async_computation | async-start | bytes 131072 | tf_op jit(solution)/shard_map/all_to_all | solution.py:213
  13.6 0.0 copy-start.1
  13.6 1.0 copy-done.1
  14.7 0.7 copy-done.3
  15.3 2.7 %pack.1.cot_hbm = bf16[128,2,8,1024]{3,2,1,0:T(8,128)(2,1)} custom-call(s32[1,128]{1,0:T(1,128)S(1)} %copy-done.3, bf16[128,2048]{1,0:T(8,128)(2,1)S(1)} %bitcast.4), custom_call_target="tpu_custom_call" | custom-call | flops 536870912 | bytes 3145728 | tf_op jit(solution)/shard_map/pack/pallas_call | solution.py:244
  18.0 4.9 %all-to-all-done.ids_ref = s32[128,1,128]{2,1,0:T(1,128)S(1)} async-done(((s32[128,1,128]{2,1,0:T(1,128)}), s32[128,1,128]{2,1,0:T(1,128)S(1)}, u32[]{:S(2)}, u32[]{:S(2)}) %all-to-all-start) | async-done | bytes 65568 | tf_op jit(solution)/shard_map/all_to_all | solution.py:213
  22.9 3.4 %rows.1 = bf16[128,2,8,1024]{3,2,1,0:T(8,128)(2,1)} custom-call(s32[128,1,128]{2,1,0:T(1,128)S(1)} %all-to-all-done.ids_ref, bf16[512,2048]{1,0:T(8,128)(2,1)S(1)} %copy-done, bf16[128,2,8,1024]{3,2,1,0:T(8,128)(2,1)} %pack.1.cot_hbm), custom_call_target="tpu_custom_call", output_to_operand_aliasing={{}: (2, {})} | custom-call | flops 2147483648 | bytes 4194304 | tf_op jit(solution)/shard_map/rows/pallas_call | solution.py:254
  26.4 5.7 %all-to-all-start.1 = ((bf16[128,2,8,1024]{3,2,1,0:T(8,128)(2,1)}), bf16[128,2,8,1024]{3,2,1,0:T(8,128)(2,1)}, u32[]{:S(2)}, u32[]{:S(2)}) async-start(bf16[128,2,8,1024]{3,2,1,0:T(8,128)(2,1)} %rows.1), calls=%async_computation.1 | async-start | bytes 8388608 | tf_op jit(solution)/shard_map/all_to_all | solution.py:213
  32.2 1.3 %prepare.1 = (bf16[512,1024]{1,0:T(8,128)(2,1)S(1)}, bf16[512,1024]{1,0:T(8,128)(2,1)S(1)}, f32[8,2048]{1,0:T(8,128)S(1)}) custom-call(s32[128,1,128]{2,1,0:T(1,128)S(1)} %all-to-all-done.ids_ref, bf16[1,2048]{1,0:T(2,128)(2,1)S(1)} %reshape.10.gain_ref), custom_call_target="tpu_custom_call" | custom-call | flops 20971520000 | bytes 2097152 | tf_op jit(solution)/shard_map/prepare/pallas_call | solution.py:266
  33.5 51.4 %all-to-all-done.1.got_hbm.cot_ref = bf16[128,2,8,1024]{3,2,1,0:T(8,128)(2,1)} async-done(((bf16[128,2,8,1024]{3,2,1,0:T(8,128)(2,1)}), bf16[128,2,8,1024]{3,2,1,0:T(8,128)(2,1)}, u32[]{:S(2)}, u32[]{:S(2)}) %all-to-all-start.1) | async-done | bytes 4194336 | tf_op jit(solution)/shard_map/all_to_all | solution.py:213
  84.9 6.0 %qkv.1 = (bf16[128,384]{1,0:T(8,128)(2,1)S(1)}, bf16[128,384]{1,0:T(8,128)(2,1)S(1)}, bf16[128,384]{1,0:T(8,128)(2,1)S(1)}, bf16[128,384]{1,0:T(8,128)(2,1)S(1)}...) custom-call(s32[1,128]{1,0:T(1,128)S(1)} %copy-done.4, ...), custom_call_target="tpu_custom_call" | custom-call | flops 1610612736 | bytes 16777216 | tf_op jit(solution)/shard_map/qkv/pallas_call | solution.py:274
  90.9 1.2 collective-permute-start
  92.1 1.2 collective-permute-start.2
  93.2 2.4 %collective-permute-start.3 = (bf16[128,384]{1,0:T(8,128)(2,1)S(1)}, bf16[128,384]{1,0:T(8,128)(2,1)S(1)}, u32[]{:S(2)}, u32[]{:S(2)}) collective-permute-start(bf16[128,384]{1,0:T(8,128)(2,1)S(1)} %get-tuple-element.20), channel_id=1, source_target_pairs={{0,4},{1,5},{2,6},{3,7},{4,0},{5,1},{6,2},{7,3},{8,12},{9,13},{10,... | collective-permute-start | bytes 294920 | tf_op jit(solution)/shard_map/ppermute | solution.py:219
  95.7 2.6 %collective-permute-start.4 = (bf16[128,384]{1,0:T(8,128)(2,1)S(1)}, bf16[128,384]{1,0:T(8,128)(2,1)S(1)}, u32[]{:S(2)}, u32[]{:S(2)}) collective-permute-start(bf16[128,384]{1,0:T(8,128)(2,1)S(1)} %get-tuple-element.21), channel_id=1, source_target_pairs={{0,5},{1,6},{2,7},{3,0},{4,1},{5,2},{6,3},{7,4},{8,13},{9,14},{10,... | collective-permute-start | bytes 294920 | tf_op jit(solution)/shard_map/ppermute | solution.py:219
  98.3 4.9 %collective-permute-done.1.refs_2_ = bf16[128,384]{1,0:T(8,128)(2,1)S(1)} collective-permute-done((bf16[128,384]{1,0:T(8,128)(2,1)S(1)}, bf16[128,384]{1,0:T(8,128)(2,1)S(1)}, u32[]{:S(2)}, u32[]{:S(2)}) %collective-permute-start.1) | collective-permute-done | bytes 98336 | tf_op jit(solution)/shard_map/ppermute | solution.py:219
  103.2 0.6 collective-permute-done.2.refs_3_
  103.9 3.4 %collective-permute-done.6.refs_7_ = bf16[128,384]{1,0:T(8,128)(2,1)S(1)} collective-permute-done((bf16[128,384]{1,0:T(8,128)(2,1)S(1)}, bf16[128,384]{1,0:T(8,128)(2,1)S(1)}, u32[]{:S(2)}, u32[]{:S(2)}) %collective-permute-start.6) | collective-permute-done | bytes 98336 | tf_op jit(solution)/shard_map/ppermute | solution.py:219
  107.3 2.5 %attention.1 = bf16[1024,128]{1,0:T(8,128)(2,1)} custom-call(bf16[128,384]{1,0:T(8,128)(2,1)S(1)} %get-tuple-element.16.refs_0_, bf16[128,384]{1,0:T(8,128)(2,1)S(1)} %collective-permute-done.refs_1_, bf16[128,384]{1,0:T(8,128)(2,1)S(1)} %collective-permute-done.1.refs_2_, bf16[128,384]{1,0:T(8,128)(2,1)S(1)} %collective-permute-done.2.refs_3_, ...), custom_call_target="tpu_custom_call" | custom-call | flops 536870912 | bytes 2097152 | tf_op jit(solution)/shard_map/attention/pallas_call | solution.py:315
  109.8 3.4 %all-to-all-start.2 = ((bf16[8,128,128]{2,1,0:T(8,128)(2,1)}), bf16[8,128,128]{2,1,0:T(8,128)(2,1)S(1)}, u32[]{:S(2)}, u32[]{:S(2)}) async-start(bf16[8,128,128]{2,1,0:T(8,128)(2,1)} %bitcast.2), calls=%async_computation.2 | async-start | bytes 524288 | tf_op jit(solution)/shard_map/all_to_all | solution.py:213
  113.2 6.2 %grad.1 = f32[512,2048]{1,0:T(8,128)} custom-call(bf16[512,1024]{1,0:T(8,128)(2,1)S(1)} %get-tuple-element.14.low_hbm.low_ref, bf16[512,1024]{1,0:T(8,128)(2,1)S(1)} %get-tuple-element.15.high_hbm.high_ref, bf16[128,2,8,1024]{3,2,1,0:T(8,128)(2,1)} %all-to-all-done.1.got_hbm.cot_ref), custom_call_target="tpu_custom_call" | custom-call | flops 2147483648 | bytes 6291456 | tf_op jit(solution)/shard_map/grad/pallas_call | solution.py:301
  119.4 0.2 copy.9
  119.6 0.8 broadcast_in_dim_reshape.3
  (18 shorter events, 0.1 us)
Async XLA Ops:
  0.6 22.3 %copy-start = (bf16[512,2048]{1,0:T(8,128)(2,1)S(1)}, bf16[512,2048]{1,0:T(8,128)(2,1)}, u32[]{:S(2)}) copy-start(bf16[512,2048]{1,0:T(8,128)(2,1)} %table_ref.1) | copy-start | bytes 6291460
  2.1 20.8 %all-to-all-start = ((s32[128,1,128]{2,1,0:T(1,128)}), s32[128,1,128]{2,1,0:T(1,128)S(1)}, u32[]{:S(2)}, u32[]{:S(2)}) async-start(s32[128,1,128]{2,1,0:T(1,128)} %spread.1), calls=%async_computation | async-start | bytes 131072 | tf_op jit(solution)/shard_map/all_to_all | solution.py:213
  13.6 1.0 copy-start.1
  14.7 0.7 copy-start.3
  26.4 5.8 %copy-start.5 = (bf16[2048]{0:T(1024)(128)(2,1)S(1)}, bf16[2048]{0:T(1024)(128)(2,1)}, u32[]{:S(2)}) copy-start(bf16[2048]{0:T(1024)(128)(2,1)} %param.10) | copy-start | bytes 12292
  26.4 58.5 %all-to-all-start.1 = ((bf16[128,2,8,1024]{3,2,1,0:T(8,128)(2,1)}), bf16[128,2,8,1024]{3,2,1,0:T(8,128)(2,1)}, u32[]{:S(2)}, u32[]{:S(2)}) async-start(bf16[128,2,8,1024]{3,2,1,0:T(8,128)(2,1)} %rows.1), calls=%async_computation.1 | async-start | bytes 8388608 | tf_op jit(solution)/shard_map/all_to_all | solution.py:213
  32.2 52.7 %copy-start.2 = (bf16[1,128,2048]{2,1,0:T(8,128)(2,1)S(1)}, bf16[1,128,2048]{2,1,0:T(8,128)(2,1)}, u32[]{:S(2)}) copy-start(bf16[1,128,2048]{2,1,0:T(8,128)(2,1)} %param.6) | copy-start | bytes 1572868
  32.2 52.7 %copy-start.4 = (s32[1,128]{1,0:T(1,128)S(1)}, s32[1,128]{1,0:T(1,128)}, u32[]{:S(2)}) copy-start(s32[1,128]{1,0:T(1,128)} %ids_ref.5) | copy-start | bytes 1540
  90.9 7.4 %collective-permute-start = (bf16[128,384]{1,0:T(8,128)(2,1)S(1)}, bf16[128,384]{1,0:T(8,128)(2,1)S(1)}, u32[]{:S(2)}, u32[]{:S(2)}) collective-permute-start(bf16[128,384]{1,0:T(8,128)(2,1)S(1)} %get-tuple-element.17), channel_id=1, source_target_pairs={{0,1},{1,2},{2,3},{3,4},{4,5},{5,6},{6,7},{7,0},{8,9},{9,10},{10,1... | collective-permute-start | bytes 294920 | tf_op jit(solution)/shard_map/ppermute | solution.py:219
  92.1 11.2 %collective-permute-start.1 = (bf16[128,384]{1,0:T(8,128)(2,1)S(1)}, bf16[128,384]{1,0:T(8,128)(2,1)S(1)}, u32[]{:S(2)}, u32[]{:S(2)}) collective-permute-start(bf16[128,384]{1,0:T(8,128)(2,1)S(1)} %get-tuple-element.18), channel_id=1, source_target_pairs={{0,2},{1,3},{2,4},{3,5},{4,6},{5,7},{6,0},{7,1},{8,10},{9,11},{10,... | collective-permute-start | bytes 294920 | tf_op jit(solution)/shard_map/ppermute | solution.py:219
  92.1 11.8 %collective-permute-start.2 = (bf16[128,384]{1,0:T(8,128)(2,1)S(1)}, bf16[128,384]{1,0:T(8,128)(2,1)S(1)}, u32[]{:S(2)}, u32[]{:S(2)}) collective-permute-start(bf16[128,384]{1,0:T(8,128)(2,1)S(1)} %get-tuple-element.19), channel_id=1, source_target_pairs={{0,3},{1,4},{2,5},{3,6},{4,7},{5,0},{6,1},{7,2},{8,11},{9,12},{10,... | collective-permute-start | bytes 294920 | tf_op jit(solution)/shard_map/ppermute | solution.py:219
  93.2 10.6 %collective-permute-start.3 = (bf16[128,384]{1,0:T(8,128)(2,1)S(1)}, bf16[128,384]{1,0:T(8,128)(2,1)S(1)}, u32[]{:S(2)}, u32[]{:S(2)}) collective-permute-start(bf16[128,384]{1,0:T(8,128)(2,1)S(1)} %get-tuple-element.20), channel_id=1, source_target_pairs={{0,4},{1,5},{2,6},{3,7},{4,0},{5,1},{6,2},{7,3},{8,12},{9,13},{10,... | collective-permute-start | bytes 294920 | tf_op jit(solution)/shard_map/ppermute | solution.py:219
  95.7 8.2 %collective-permute-start.4 = (bf16[128,384]{1,0:T(8,128)(2,1)S(1)}, bf16[128,384]{1,0:T(8,128)(2,1)S(1)}, u32[]{:S(2)}, u32[]{:S(2)}) collective-permute-start(bf16[128,384]{1,0:T(8,128)(2,1)S(1)} %get-tuple-element.21), channel_id=1, source_target_pairs={{0,5},{1,6},{2,7},{3,0},{4,1},{5,2},{6,3},{7,4},{8,13},{9,14},{10,... | collective-permute-start | bytes 294920 | tf_op jit(solution)/shard_map/ppermute | solution.py:219
  98.3 5.6 %collective-permute-start.5 = (bf16[128,384]{1,0:T(8,128)(2,1)S(1)}, bf16[128,384]{1,0:T(8,128)(2,1)S(1)}, u32[]{:S(2)}, u32[]{:S(2)}) collective-permute-start(bf16[128,384]{1,0:T(8,128)(2,1)S(1)} %get-tuple-element.22), channel_id=1, source_target_pairs={{0,6},{1,7},{2,0},{3,1},{4,2},{5,3},{6,4},{7,5},{8,14},{9,15},{10,... | collective-permute-start | bytes 294920 | tf_op jit(solution)/shard_map/ppermute | solution.py:219
  103.2 4.0 %collective-permute-start.6 = (bf16[128,384]{1,0:T(8,128)(2,1)S(1)}, bf16[128,384]{1,0:T(8,128)(2,1)S(1)}, u32[]{:S(2)}, u32[]{:S(2)}) collective-permute-start(bf16[128,384]{1,0:T(8,128)(2,1)S(1)} %get-tuple-element.23), channel_id=1, source_target_pairs={{0,7},{1,0},{2,1},{3,2},{4,3},{5,4},{6,5},{7,6},{8,15},{9,8},{10,9... | collective-permute-start | bytes 294920 | tf_op jit(solution)/shard_map/ppermute | solution.py:219
  109.8 9.6 %all-to-all-start.2 = ((bf16[8,128,128]{2,1,0:T(8,128)(2,1)}), bf16[8,128,128]{2,1,0:T(8,128)(2,1)S(1)}, u32[]{:S(2)}, u32[]{:S(2)}) async-start(bf16[8,128,128]{2,1,0:T(8,128)(2,1)} %bitcast.2), calls=%async_computation.2 | async-start | bytes 524288 | tf_op jit(solution)/shard_map/all_to_all | solution.py:213

commit v5 on v4

--- a/solution.py
+++ b/solution.py
@@ -171,7 +171,7 @@
 
 
 def attention_kernel(block, *refs):
-    *ins, mixed_ref, qkv_ref = refs
+    *ins, mixed_hbm, qkv_ref, mixed_ref, sems = refs
     tokens = ins[0].shape[0]
     seq = tokens * HEADS
     me = lax.axis_index("ctx")
@@ -180,6 +180,7 @@
         qkv_ref[pl.ds(pl.multiple_of(source * tokens, tokens), tokens), :] = ref[...]
     lanes = (((1,), (1,)), ((), ()))
     allowed = iota((block, block), 1) <= iota((block, block), 0)
+    stores = []
     for i in range(seq // block):
         here = slice(i * block, (i + 1) * block)
         query = qkv_ref[here, :HEAD]
@@ -197,6 +198,17 @@
             total += jnp.sum(weights, axis=1, keepdims=True)
             mixed += dot(weights.astype(jnp.bfloat16), qkv_ref[: i * block, 2 * HEAD :])
         mixed_ref[here, :] = (mixed / total).astype(jnp.bfloat16)
+        stores.append(
+            pltpu.make_async_copy(mixed_ref.at[here], mixed_hbm.at[here], sems.at[i])
+        )
+        stores[-1].start()
+    for store in stores:
+        store.wait()
+
+
+def join_kernel(heads_ref, out_ref):
+    for h in range(HEADS):
+        out_ref[:, h * HEAD : (h + 1) * HEAD] = heads_ref[h]
 
 
 def call(kernel, out, flops, moved, mb=24, **kwargs):
@@ -235,9 +247,11 @@
     whole = pl.BlockSpec(memory_space=pltpu.VMEM)
     remote = pl.BlockSpec(memory_space=pltpu.HBM)
 
-    near_hbm = pltpu.with_memory_space_constraint(ngram_ids, pltpu.HBM)
     all_ids = exchange(
-        call(spread_kernel, shape((owners, 1, tokens), jnp.int32), 0, 0, name="spread")(near_hbm), BOTH
+        call(spread_kernel, pltpu.VMEM((owners, 1, tokens), jnp.int32), 0, 0, name="spread")(
+            ngram_ids
+        ),
+        BOTH,
     )
     blocks = pltpu.HBM((owners, 2, TILE, HALF), bf16)
     stage = pltpu.VMEM((owners, TILE, HALF), bf16)
@@ -314,14 +328,22 @@
     )(low, high, got)
     mixed = call(
         functools.partial(attention_kernel, 256),
-        shape((ctx * tokens, HEAD), bf16),
+        pltpu.HBM((ctx * tokens, HEAD), bf16),
         4 * ctx * tokens * ctx * tokens * HEAD,
         2 * MB,
         name="attention",
-        scratch_shapes=[pltpu.VMEM((ctx * tokens, 3 * HEAD), bf16)],
+        in_specs=[whole] * HEADS,
+        out_specs=remote,
+        scratch_shapes=[
+            pltpu.VMEM((ctx * tokens, 3 * HEAD), bf16),
+            pltpu.VMEM((ctx * tokens, HEAD), bf16),
+            pltpu.SemaphoreType.DMA((ctx * tokens // 256,)),
+        ],
     )(*shift_all(qkv))
     context = exchange(mixed.reshape(ctx, tokens, HEAD), "ctx")
-    context = context.transpose(1, 0, 2).reshape(tokens, HEADS * HEAD)
+    context = call(
+        join_kernel, shape((tokens, HEADS * HEAD), bf16), 0, MB // 2, name="join"
+    )(context)
     return (context[None], table_grad)
 
 

time: 121 us -> 121 us (level)
    unnamed x12 -> x14, local copies, waits for them, and re-layouts: 1.71 us -> 2.51 us
    pallas_call x2 -> x3, Pallas kernels: 4.01 us -> 3.93 us  [the longest x1 2.5 us: shards(): call(functools.partial(attention_kernel, 256), pltpu.HBM((ctx * tokens, H...]
where the time goes in v5:
time: 121 us; the launch traced here: 120 us
  waiting for transfers between devices  65.3 us (54%)
  starting transfers between devices  28 us (23%)
  Pallas kernels  23.5 us (19%)
  local copies, waits for them, and re-layouts  2.52 us (2%)
    all_to_all x3, waiting for transfers between devices, exchange(): return lax.all_to_all(x, axes, split_axis=0, concat_axis=0, tiled=True)  56.3 us
    all_to_all x3, starting transfers between devices, exchange(): return lax.all_to_all(x, axes, split_axis=0, concat_axis=0, tiled=True)  20.6 us
    ppermute x7, waiting for transfers between devices, shift_all(): lax.ppermute(pieces[k], 'ctx', [(i, (i + k) % n) for i in range(n)])  8.98 us
    ppermute x7, starting transfers between devices, shift_all(): lax.ppermute(pieces[k], 'ctx', [(i, (i + k) % n) for i in range(n)])  7.43 us
    pallas_call x1, Pallas kernels, shards(): call(grad_kernel, shape((held, width), f32), 2 * slots * held * width, 6...  6.19 us
    pallas_call x1, Pallas kernels, shards(): call(functools.partial(qkv_kernel, held), [shape((tokens, 3 * HEAD), bf16...  5.96 us
    pallas_call x1, Pallas kernels, shards(): call(rows_kernel, blocks, 2 * slots * held * width, 4 * MB, name='rows',...  3.42 us
    pallas_call x1, Pallas kernels, shards(): call(functools.partial(pack_kernel, held), blocks, 2 * slots * tokens * w...  2.68 us
  transfers between devices with their start and end apart: 10, of which 5 were waited for; matrix products, arithmetic and copies ran while one was open for 0% of the time, Pallas kernels for 8%

profile of v5, /device:TPU:1, one launch (start us, length us, event | category | flops | bytes accessed | tf_op | source)
XLA Modules:
  0.0 120.1 jit_solution(3202125644743509740)
XLA Ops:
  0.6 0.0 copy-start.3
  0.7 0.8 copy-done.3
  1.4 0.7 spread.1
  2.1 11.5 %all-to-all-start = ((s32[128,1,128]{2,1,0:T(1,128)}), s32[128,1,128]{2,1,0:T(1,128)S(1)}, u32[]{:S(2)}, u32[]{:S(2)}) async-start(s32[128,1,128]{2,1,0:T(1,128)} %spread.1), calls=%async_computation | async-start | bytes 131072 | tf_op jit(solution)/shard_map/all_to_all | solution.py:225
  13.6 1.0 copy-done.1
  14.7 0.7 copy-done.4
  15.3 2.7 %pack.1.cot_hbm = bf16[128,2,8,1024]{3,2,1,0:T(8,128)(2,1)} custom-call(s32[1,128]{1,0:T(1,128)S(1)} %copy-done.4, bf16[128,2048]{1,0:T(8,128)(2,1)S(1)} %bitcast.4), custom_call_target="tpu_custom_call" | custom-call | flops 536870912 | bytes 3145728 | tf_op jit(solution)/shard_map/pack/pallas_call | solution.py:258
  18.0 4.9 %all-to-all-done.ids_ref = s32[128,1,128]{2,1,0:T(1,128)S(1)} async-done(((s32[128,1,128]{2,1,0:T(1,128)}), s32[128,1,128]{2,1,0:T(1,128)S(1)}, u32[]{:S(2)}, u32[]{:S(2)}) %all-to-all-start) | async-done | bytes 65568 | tf_op jit(solution)/shard_map/all_to_all | solution.py:225
  22.9 3.4 %rows.1 = bf16[128,2,8,1024]{3,2,1,0:T(8,128)(2,1)} custom-call(s32[128,1,128]{2,1,0:T(1,128)S(1)} %all-to-all-done.ids_ref, bf16[512,2048]{1,0:T(8,128)(2,1)S(1)} %copy-done, bf16[128,2,8,1024]{3,2,1,0:T(8,128)(2,1)} %pack.1.cot_hbm), custom_call_target="tpu_custom_call", output_to_operand_aliasing={{}: (2, {})} | custom-call | flops 2147483648 | bytes 4194304 | tf_op jit(solution)/shard_map/rows/pallas_call | solution.py:268
  26.4 5.7 %all-to-all-start.1 = ((bf16[128,2,8,1024]{3,2,1,0:T(8,128)(2,1)}), bf16[128,2,8,1024]{3,2,1,0:T(8,128)(2,1)}, u32[]{:S(2)}, u32[]{:S(2)}) async-start(bf16[128,2,8,1024]{3,2,1,0:T(8,128)(2,1)} %rows.1), calls=%async_computation.1 | async-start | bytes 8388608 | tf_op jit(solution)/shard_map/all_to_all | solution.py:225
  32.2 1.3 %prepare.1 = (bf16[512,1024]{1,0:T(8,128)(2,1)S(1)}, bf16[512,1024]{1,0:T(8,128)(2,1)S(1)}, f32[8,2048]{1,0:T(8,128)S(1)}) custom-call(s32[128,1,128]{2,1,0:T(1,128)S(1)} %all-to-all-done.ids_ref, bf16[1,2048]{1,0:T(2,128)(2,1)S(1)} %reshape.10.gain_ref), custom_call_target="tpu_custom_call" | custom-call | flops 20971520000 | bytes 2097152 | tf_op jit(solution)/shard_map/prepare/pallas_call | solution.py:280
  33.5 51.4 %all-to-all-done.1.got_hbm.cot_ref = bf16[128,2,8,1024]{3,2,1,0:T(8,128)(2,1)} async-done(((bf16[128,2,8,1024]{3,2,1,0:T(8,128)(2,1)}), bf16[128,2,8,1024]{3,2,1,0:T(8,128)(2,1)}, u32[]{:S(2)}, u32[]{:S(2)}) %all-to-all-start.1) | async-done | bytes 4194336 | tf_op jit(solution)/shard_map/all_to_all | solution.py:225
  84.9 6.0 %qkv.1 = (bf16[128,384]{1,0:T(8,128)(2,1)S(1)}, bf16[128,384]{1,0:T(8,128)(2,1)S(1)}, bf16[128,384]{1,0:T(8,128)(2,1)S(1)}, bf16[128,384]{1,0:T(8,128)(2,1)S(1)}...) custom-call(s32[1,128]{1,0:T(1,128)S(1)} %copy-done.5, ...), custom_call_target="tpu_custom_call" | custom-call | flops 1610612736 | bytes 16777216 | tf_op jit(solution)/shard_map/qkv/pallas_call | solution.py:288
  90.9 1.2 collective-permute-start
  92.1 1.2 collective-permute-start.2
  93.2 2.4 %collective-permute-start.3 = (bf16[128,384]{1,0:T(8,128)(2,1)S(1)}, bf16[128,384]{1,0:T(8,128)(2,1)S(1)}, u32[]{:S(2)}, u32[]{:S(2)}) collective-permute-start(bf16[128,384]{1,0:T(8,128)(2,1)S(1)} %get-tuple-element.20), channel_id=1, source_target_pairs={{0,4},{1,5},{2,6},{3,7},{4,0},{5,1},{6,2},{7,3},{8,12},{9,13},{10,... | collective-permute-start | bytes 294920 | tf_op jit(solution)/shard_map/ppermute | solution.py:231
  95.7 2.6 %collective-permute-start.4 = (bf16[128,384]{1,0:T(8,128)(2,1)S(1)}, bf16[128,384]{1,0:T(8,128)(2,1)S(1)}, u32[]{:S(2)}, u32[]{:S(2)}) collective-permute-start(bf16[128,384]{1,0:T(8,128)(2,1)S(1)} %get-tuple-element.21), channel_id=1, source_target_pairs={{0,5},{1,6},{2,7},{3,0},{4,1},{5,2},{6,3},{7,4},{8,13},{9,14},{10,... | collective-permute-start | bytes 294920 | tf_op jit(solution)/shard_map/ppermute | solution.py:231
  98.3 4.9 %collective-permute-done.1.refs_2_ = bf16[128,384]{1,0:T(8,128)(2,1)S(1)} collective-permute-done((bf16[128,384]{1,0:T(8,128)(2,1)S(1)}, bf16[128,384]{1,0:T(8,128)(2,1)S(1)}, u32[]{:S(2)}, u32[]{:S(2)}) %collective-permute-start.1) | collective-permute-done | bytes 98336 | tf_op jit(solution)/shard_map/ppermute | solution.py:231
  103.2 0.6 collective-permute-done.2.refs_3_
  103.9 3.4 %collective-permute-done.6.refs_7_ = bf16[128,384]{1,0:T(8,128)(2,1)S(1)} collective-permute-done((bf16[128,384]{1,0:T(8,128)(2,1)S(1)}, bf16[128,384]{1,0:T(8,128)(2,1)S(1)}, u32[]{:S(2)}, u32[]{:S(2)}) %collective-permute-start.6) | collective-permute-done | bytes 98336 | tf_op jit(solution)/shard_map/ppermute | solution.py:231
  107.3 2.5 %attention.1 = bf16[1024,128]{1,0:T(8,128)(2,1)} custom-call(bf16[128,384]{1,0:T(8,128)(2,1)S(1)} %get-tuple-element.16.refs_0_, bf16[128,384]{1,0:T(8,128)(2,1)S(1)} %collective-permute-done.refs_1_, bf16[128,384]{1,0:T(8,128)(2,1)S(1)} %collective-permute-done.1.refs_2_, bf16[128,384]{1,0:T(8,128)(2,1)S(1)} %collective-permute-done.2.refs_3_, ...), custom_call_target="tpu_custom_call" | custom-call | flops 536870912 | bytes 2097152 | tf_op jit(solution)/shard_map/attention/pallas_call | solution.py:329
  109.8 3.4 %all-to-all-start.2 = ((bf16[8,128,128]{2,1,0:T(8,128)(2,1)}), bf16[8,128,128]{2,1,0:T(8,128)(2,1)S(1)}, u32[]{:S(2)}, u32[]{:S(2)}) async-start(bf16[8,128,128]{2,1,0:T(8,128)(2,1)} %bitcast.6), calls=%async_computation.2 | async-start | bytes 524288 | tf_op jit(solution)/shard_map/all_to_all | solution.py:225
  113.2 6.2 %grad.1 = f32[512,2048]{1,0:T(8,128)} custom-call(bf16[512,1024]{1,0:T(8,128)(2,1)S(1)} %get-tuple-element.14.low_hbm.low_ref, bf16[512,1024]{1,0:T(8,128)(2,1)S(1)} %get-tuple-element.15.high_hbm.high_ref, bf16[128,2,8,1024]{3,2,1,0:T(8,128)(2,1)} %all-to-all-done.1.got_hbm.cot_ref), custom_call_target="tpu_custom_call" | custom-call | flops 2147483648 | bytes 6291456 | tf_op jit(solution)/shard_map/grad/pallas_call | solution.py:315
  119.4 0.8 join.1
  (19 shorter events, 0.1 us)
Async XLA Ops:
  0.6 22.3 %copy-start = (bf16[512,2048]{1,0:T(8,128)(2,1)S(1)}, bf16[512,2048]{1,0:T(8,128)(2,1)}, u32[]{:S(2)}) copy-start(bf16[512,2048]{1,0:T(8,128)(2,1)} %table_ref.1) | copy-start | bytes 6291460
  0.6 0.8 copy-start.3
  2.1 20.8 %all-to-all-start = ((s32[128,1,128]{2,1,0:T(1,128)}), s32[128,1,128]{2,1,0:T(1,128)S(1)}, u32[]{:S(2)}, u32[]{:S(2)}) async-start(s32[128,1,128]{2,1,0:T(1,128)} %spread.1), calls=%async_computation | async-start | bytes 131072 | tf_op jit(solution)/shard_map/all_to_all | solution.py:225
  13.6 1.0 copy-start.1
  14.7 0.7 copy-start.4
  26.4 5.8 %copy-start.6 = (bf16[2048]{0:T(1024)(128)(2,1)S(1)}, bf16[2048]{0:T(1024)(128)(2,1)}, u32[]{:S(2)}) copy-start(bf16[2048]{0:T(1024)(128)(2,1)} %param.10) | copy-start | bytes 12292
  26.4 58.5 %all-to-all-start.1 = ((bf16[128,2,8,1024]{3,2,1,0:T(8,128)(2,1)}), bf16[128,2,8,1024]{3,2,1,0:T(8,128)(2,1)}, u32[]{:S(2)}, u32[]{:S(2)}) async-start(bf16[128,2,8,1024]{3,2,1,0:T(8,128)(2,1)} %rows.1), calls=%async_computation.1 | async-start | bytes 8388608 | tf_op jit(solution)/shard_map/all_to_all | solution.py:225
  32.2 52.7 %copy-start.2 = (bf16[1,128,2048]{2,1,0:T(8,128)(2,1)S(1)}, bf16[1,128,2048]{2,1,0:T(8,128)(2,1)}, u32[]{:S(2)}) copy-start(bf16[1,128,2048]{2,1,0:T(8,128)(2,1)} %param.6) | copy-start | bytes 1572868
  32.2 52.7 %copy-start.5 = (s32[1,128]{1,0:T(1,128)S(1)}, s32[1,128]{1,0:T(1,128)}, u32[]{:S(2)}) copy-start(s32[1,128]{1,0:T(1,128)} %ids_ref.5) | copy-start | bytes 1540
  90.9 7.4 %collective-permute-start = (bf16[128,384]{1,0:T(8,128)(2,1)S(1)}, bf16[128,384]{1,0:T(8,128)(2,1)S(1)}, u32[]{:S(2)}, u32[]{:S(2)}) collective-permute-start(bf16[128,384]{1,0:T(8,128)(2,1)S(1)} %get-tuple-element.17), channel_id=1, source_target_pairs={{0,1},{1,2},{2,3},{3,4},{4,5},{5,6},{6,7},{7,0},{8,9},{9,10},{10,1... | collective-permute-start | bytes 294920 | tf_op jit(solution)/shard_map/ppermute | solution.py:231
  92.1 11.2 %collective-permute-start.1 = (bf16[128,384]{1,0:T(8,128)(2,1)S(1)}, bf16[128,384]{1,0:T(8,128)(2,1)S(1)}, u32[]{:S(2)}, u32[]{:S(2)}) collective-permute-start(bf16[128,384]{1,0:T(8,128)(2,1)S(1)} %get-tuple-element.18), channel_id=1, source_target_pairs={{0,2},{1,3},{2,4},{3,5},{4,6},{5,7},{6,0},{7,1},{8,10},{9,11},{10,... | collective-permute-start | bytes 294920 | tf_op jit(solution)/shard_map/ppermute | solution.py:231
  92.1 11.8 %collective-permute-start.2 = (bf16[128,384]{1,0:T(8,128)(2,1)S(1)}, bf16[128,384]{1,0:T(8,128)(2,1)S(1)}, u32[]{:S(2)}, u32[]{:S(2)}) collective-permute-start(bf16[128,384]{1,0:T(8,128)(2,1)S(1)} %get-tuple-element.19), channel_id=1, source_target_pairs={{0,3},{1,4},{2,5},{3,6},{4,7},{5,0},{6,1},{7,2},{8,11},{9,12},{10,... | collective-permute-start | bytes 294920 | tf_op jit(solution)/shard_map/ppermute | solution.py:231
  93.2 10.6 %collective-permute-start.3 = (bf16[128,384]{1,0:T(8,128)(2,1)S(1)}, bf16[128,384]{1,0:T(8,128)(2,1)S(1)}, u32[]{:S(2)}, u32[]{:S(2)}) collective-permute-start(bf16[128,384]{1,0:T(8,128)(2,1)S(1)} %get-tuple-element.20), channel_id=1, source_target_pairs={{0,4},{1,5},{2,6},{3,7},{4,0},{5,1},{6,2},{7,3},{8,12},{9,13},{10,... | collective-permute-start | bytes 294920 | tf_op jit(solution)/shard_map/ppermute | solution.py:231
  95.7 8.2 %collective-permute-start.4 = (bf16[128,384]{1,0:T(8,128)(2,1)S(1)}, bf16[128,384]{1,0:T(8,128)(2,1)S(1)}, u32[]{:S(2)}, u32[]{:S(2)}) collective-permute-start(bf16[128,384]{1,0:T(8,128)(2,1)S(1)} %get-tuple-element.21), channel_id=1, source_target_pairs={{0,5},{1,6},{2,7},{3,0},{4,1},{5,2},{6,3},{7,4},{8,13},{9,14},{10,... | collective-permute-start | bytes 294920 | tf_op jit(solution)/shard_map/ppermute | solution.py:231
  98.3 5.6 %collective-permute-start.5 = (bf16[128,384]{1,0:T(8,128)(2,1)S(1)}, bf16[128,384]{1,0:T(8,128)(2,1)S(1)}, u32[]{:S(2)}, u32[]{:S(2)}) collective-permute-start(bf16[128,384]{1,0:T(8,128)(2,1)S(1)} %get-tuple-element.22), channel_id=1, source_target_pairs={{0,6},{1,7},{2,0},{3,1},{4,2},{5,3},{6,4},{7,5},{8,14},{9,15},{10,... | collective-permute-start | bytes 294920 | tf_op jit(solution)/shard_map/ppermute | solution.py:231
  103.2 4.0 %collective-permute-start.6 = (bf16[128,384]{1,0:T(8,128)(2,1)S(1)}, bf16[128,384]{1,0:T(8,128)(2,1)S(1)}, u32[]{:S(2)}, u32[]{:S(2)}) collective-permute-start(bf16[128,384]{1,0:T(8,128)(2,1)S(1)} %get-tuple-element.23), channel_id=1, source_target_pairs={{0,7},{1,0},{2,1},{3,2},{4,3},{5,4},{6,5},{7,6},{8,15},{9,8},{10,9... | collective-permute-start | bytes 294920 | tf_op jit(solution)/shard_map/ppermute | solution.py:231
  109.8 9.6 %all-to-all-start.2 = ((bf16[8,128,128]{2,1,0:T(8,128)(2,1)}), bf16[8,128,128]{2,1,0:T(8,128)(2,1)S(1)}, u32[]{:S(2)}, u32[]{:S(2)}) async-start(bf16[8,128,128]{2,1,0:T(8,128)(2,1)} %bitcast.6), calls=%async_computation.2 | async-start | bytes 524288 | tf_op jit(solution)/shard_map/all_to_all | solution.py:225

commit v6 on v5

--- a/solution.py
+++ b/solution.py
@@ -14,7 +14,7 @@
 HALF = 1024
 MB = 1024 * 1024
 AHEAD = 4
-BOTH = ("table", "ctx")
+BOTH = ("ctx", "table")
 
 
 def iota(shape, dim):
@@ -33,6 +33,11 @@
     n = ids.shape[1]
     owner = jnp.broadcast_to(ids, (n, n)) // held
     return owner, owner.astype(jnp.float32).T.astype(jnp.int32)
+
+
+def position(owner):
+    ctx = lax.axis_size("ctx")
+    return owner % ctx * lax.axis_size("table") + owner // ctx
 
 
 def asked_rows(ids_ref, held):
@@ -52,7 +57,7 @@
     own_lane, own_sub = owner_grid(ids_ref[...], held)
     earlier = iota((tokens, tokens), 0) < iota((tokens, tokens), 1)
     rank = jnp.sum(jnp.where((own_lane == own_sub) & earlier, 1, 0), axis=0, keepdims=True)
-    slot = own_lane[0:1] * TILE + rank
+    slot = position(own_lane[0:1]) * TILE + rank
     at = iota((stage_ref.shape[0] * TILE, tokens), 0)
     made = dot(onehot(at == slot), cot_ref[:, :HALF]) + dot(onehot(at == slot + CAP), cot_ref[:, HALF:])
     stage_ref[...] = made.astype(jnp.bfloat16).reshape(stage_ref.shape)
@@ -133,7 +138,7 @@
     own_lane, own_sub = owner_grid(ids_ref[...], held)
     same = (own_lane == own_sub) & (iota((n, n), 1) < iota((n, n), 0))
     rank = jnp.sum(jnp.where(same, 1, 0), axis=1, keepdims=True)
-    slot = own_sub[:, 0:1] * TILE + rank
+    slot = position(own_sub[:, 0:1]) * TILE + rank
     pick = onehot(iota((2 * n, slots), 1) == jnp.concatenate([slot, slot + CAP], axis=0))
     load.wait()
     rows = dot(pick, got_ref[...].reshape(slots, HALF))

time: 121 us -> 118 us (0.975)
  waiting for transfers between devices: 65.3 us -> 61.4 us
    ppermute x7, waiting for transfers between devices: 8.98 us -> 5.62 us  [shift_all(): lax.ppermute(pieces[k], 'ctx', [(i, (i + k) % n) for i in range(n)])]
  transfers between devices with their start and end apart: 10 -> 10, of which waited for: 5 -> 8; matrix products, arithmetic and copies ran while one was open for 0% -> 0% of each run, Pallas kernels for 8% -> 9%
where the time goes in v6:
time: 118 us; the launch traced here: 117 us
  waiting for transfers between devices  61.4 us (52%)
  starting transfers between devices  29.1 us (25%)
  Pallas kernels  23.4 us (20%)
  local copies, waits for them, and re-layouts  2.52 us (2%)
    all_to_all x3, waiting for transfers between devices, exchange(): return lax.all_to_all(x, axes, split_axis=0, concat_axis=0, tiled=True)  55.8 us
    all_to_all x3, starting transfers between devices, exchange(): return lax.all_to_all(x, axes, split_axis=0, concat_axis=0, tiled=True)  21.3 us
    ppermute x7, starting transfers between devices, shift_all(): lax.ppermute(pieces[k], 'ctx', [(i, (i + k) % n) for i in range(n)])  7.83 us
    pallas_call x1, Pallas kernels, shards(): call(grad_kernel, shape((held, width), f32), 2 * slots * held * width, 6...  6.17 us
    pallas_call x1, Pallas kernels, shards(): call(functools.partial(qkv_kernel, held), [shape((tokens, 3 * HEAD), bf16...  5.96 us
    ppermute x7, waiting for transfers between devices, shift_all(): lax.ppermute(pieces[k], 'ctx', [(i, (i + k) % n) for i in range(n)])  5.62 us
    pallas_call x1, Pallas kernels, shards(): call(rows_kernel, blocks, 2 * slots * held * width, 4 * MB, name='rows',...  3.42 us
    pallas_call x1, Pallas kernels, shards(): call(functools.partial(pack_kernel, held), blocks, 2 * slots * tokens * w...  2.68 us
  transfers between devices with their start and end apart: 10, of which 8 were waited for; matrix products, arithmetic and copies ran while one was open for 0% of the time, Pallas kernels for 9%

profile of v6, /device:TPU:1, one launch (start us, length us, event | category | flops | bytes accessed | tf_op | source)
XLA Modules:
  0.0 117.2 jit_solution(1250206402213308266)
XLA Ops:
  0.7 0.8 copy-done.3
  1.4 0.7 spread.1
  2.1 11.5 %all-to-all-start = ((s32[128,1,128]{2,1,0:T(1,128)}), s32[128,1,128]{2,1,0:T(1,128)S(1)}, u32[]{:S(2)}, u32[]{:S(2)}) async-start(s32[128,1,128]{2,1,0:T(1,128)} %spread.1), calls=%async_computation | async-start | bytes 131072 | tf_op jit(solution)/shard_map/all_to_all | solution.py:230
  13.6 1.0 copy-done.1
  14.7 0.7 copy-done.4
  15.3 2.7 %pack.1.cot_hbm = bf16[128,2,8,1024]{3,2,1,0:T(8,128)(2,1)} custom-call(s32[1,128]{1,0:T(1,128)S(1)} %copy-done.4, bf16[128,2048]{1,0:T(8,128)(2,1)S(1)} %bitcast.4), custom_call_target="tpu_custom_call" | custom-call | flops 536870912 | bytes 3145728 | tf_op jit(solution)/shard_map/pack/pallas_call | solution.py:263
  18.0 5.1 %all-to-all-done.ids_ref = s32[128,1,128]{2,1,0:T(1,128)S(1)} async-done(((s32[128,1,128]{2,1,0:T(1,128)}), s32[128,1,128]{2,1,0:T(1,128)S(1)}, u32[]{:S(2)}, u32[]{:S(2)}) %all-to-all-start) | async-done | bytes 65568 | tf_op jit(solution)/shard_map/all_to_all | solution.py:230
  23.1 3.4 %rows.1 = bf16[128,2,8,1024]{3,2,1,0:T(8,128)(2,1)} custom-call(s32[128,1,128]{2,1,0:T(1,128)S(1)} %all-to-all-done.ids_ref, bf16[512,2048]{1,0:T(8,128)(2,1)S(1)} %copy-done, bf16[128,2,8,1024]{3,2,1,0:T(8,128)(2,1)} %pack.1.cot_hbm), custom_call_target="tpu_custom_call", output_to_operand_aliasing={{}: (2, {})} | custom-call | flops 2147483648 | bytes 4194304 | tf_op jit(solution)/shard_map/rows/pallas_call | solution.py:273
  26.6 5.5 %all-to-all-start.1 = ((bf16[128,2,8,1024]{3,2,1,0:T(8,128)(2,1)}), bf16[128,2,8,1024]{3,2,1,0:T(8,128)(2,1)}, u32[]{:S(2)}, u32[]{:S(2)}) async-start(bf16[128,2,8,1024]{3,2,1,0:T(8,128)(2,1)} %rows.1), calls=%async_computation.1 | async-start | bytes 8388608 | tf_op jit(solution)/shard_map/all_to_all | solution.py:230
  32.2 1.3 %prepare.1 = (bf16[512,1024]{1,0:T(8,128)(2,1)S(1)}, bf16[512,1024]{1,0:T(8,128)(2,1)S(1)}, f32[8,2048]{1,0:T(8,128)S(1)}) custom-call(s32[128,1,128]{2,1,0:T(1,128)S(1)} %all-to-all-done.ids_ref, bf16[1,2048]{1,0:T(2,128)(2,1)S(1)} %reshape.10.gain_ref), custom_call_target="tpu_custom_call" | custom-call | flops 20971520000 | bytes 2097152 | tf_op jit(solution)/shard_map/prepare/pallas_call | solution.py:285
  33.5 50.3 %all-to-all-done.1.got_hbm.cot_ref = bf16[128,2,8,1024]{3,2,1,0:T(8,128)(2,1)} async-done(((bf16[128,2,8,1024]{3,2,1,0:T(8,128)(2,1)}), bf16[128,2,8,1024]{3,2,1,0:T(8,128)(2,1)}, u32[]{:S(2)}, u32[]{:S(2)}) %all-to-all-start.1) | async-done | bytes 4194336 | tf_op jit(solution)/shard_map/all_to_all | solution.py:230
  83.8 6.0 %qkv.1 = (bf16[128,384]{1,0:T(8,128)(2,1)S(1)}, bf16[128,384]{1,0:T(8,128)(2,1)S(1)}, bf16[128,384]{1,0:T(8,128)(2,1)S(1)}, bf16[128,384]{1,0:T(8,128)(2,1)S(1)}...) custom-call(s32[1,128]{1,0:T(1,128)S(1)} %copy-done.5, ...), custom_call_target="tpu_custom_call" | custom-call | flops 1610612736 | bytes 16777216 | tf_op jit(solution)/shard_map/qkv/pallas_call | solution.py:293
  89.7 0.7 collective-permute-start
  90.5 1.1 collective-permute-start.1
  91.5 1.8 %collective-permute-start.2 = (bf16[128,384]{1,0:T(8,128)(2,1)S(1)}, bf16[128,384]{1,0:T(8,128)(2,1)S(1)}, u32[]{:S(2)}, u32[]{:S(2)}) collective-permute-start(bf16[128,384]{1,0:T(8,128)(2,1)S(1)} %get-tuple-element.19), channel_id=1, source_target_pairs={{0,3},{1,4},{2,5},{3,6},{4,7},{5,0},{6,1},{7,2},{8,11},{9,12},{10,... | collective-permute-start | bytes 294920 | tf_op jit(solution)/shard_map/ppermute | solution.py:236
  93.8 2.6 %collective-permute-start.4 = (bf16[128,384]{1,0:T(8,128)(2,1)S(1)}, bf16[128,384]{1,0:T(8,128)(2,1)S(1)}, u32[]{:S(2)}, u32[]{:S(2)}) collective-permute-start(bf16[128,384]{1,0:T(8,128)(2,1)S(1)} %get-tuple-element.21), channel_id=1, source_target_pairs={{0,5},{1,6},{2,7},{3,0},{4,1},{5,2},{6,3},{7,4},{8,13},{9,14},{10,... | collective-permute-start | bytes 294920 | tf_op jit(solution)/shard_map/ppermute | solution.py:236
  96.9 1.1 collective-permute-start.6
  98.2 3.6 %collective-permute-done.3.refs_4_ = bf16[128,384]{1,0:T(8,128)(2,1)S(1)} collective-permute-done((bf16[128,384]{1,0:T(8,128)(2,1)S(1)}, bf16[128,384]{1,0:T(8,128)(2,1)S(1)}, u32[]{:S(2)}, u32[]{:S(2)}) %collective-permute-start.3) | collective-permute-done | bytes 98336 | tf_op jit(solution)/shard_map/ppermute | solution.py:236
  101.8 0.6 collective-permute-done.4.refs_5_
  102.4 0.8 collective-permute-done.6.refs_7_
  103.2 2.5 %attention.1 = bf16[1024,128]{1,0:T(8,128)(2,1)} custom-call(bf16[128,384]{1,0:T(8,128)(2,1)S(1)} %get-tuple-element.16.refs_0_, bf16[128,384]{1,0:T(8,128)(2,1)S(1)} %collective-permute-done.refs_1_, bf16[128,384]{1,0:T(8,128)(2,1)S(1)} %collective-permute-done.1.refs_2_, bf16[128,384]{1,0:T(8,128)(2,1)S(1)} %collective-permute-done.2.refs_3_, ...), custom_call_target="tpu_custom_call" | custom-call | flops 536870912 | bytes 2097152 | tf_op jit(solution)/shard_map/attention/pallas_call | solution.py:334
  105.7 4.3 %all-to-all-start.2 = ((bf16[8,128,128]{2,1,0:T(8,128)(2,1)}), bf16[8,128,128]{2,1,0:T(8,128)(2,1)S(1)}, u32[]{:S(2)}, u32[]{:S(2)}) async-start(bf16[8,128,128]{2,1,0:T(8,128)(2,1)} %bitcast.6), calls=%async_computation.2 | async-start | bytes 524288 | tf_op jit(solution)/shard_map/all_to_all | solution.py:230
  110.0 6.2 %grad.1 = f32[512,2048]{1,0:T(8,128)} custom-call(bf16[512,1024]{1,0:T(8,128)(2,1)S(1)} %get-tuple-element.14.low_hbm.low_ref, bf16[512,1024]{1,0:T(8,128)(2,1)S(1)} %get-tuple-element.15.high_hbm.high_ref, bf16[128,2,8,1024]{3,2,1,0:T(8,128)(2,1)} %all-to-all-done.1.got_hbm.cot_ref), custom_call_target="tpu_custom_call" | custom-call | flops 2147483648 | bytes 6291456 | tf_op jit(solution)/shard_map/grad/pallas_call | solution.py:320
  116.5 0.8 join.1
  (19 shorter events, 1.5 us)
Async XLA Ops:
  0.6 22.5 %copy-start = (bf16[512,2048]{1,0:T(8,128)(2,1)S(1)}, bf16[512,2048]{1,0:T(8,128)(2,1)}, u32[]{:S(2)}) copy-start(bf16[512,2048]{1,0:T(8,128)(2,1)} %table_ref.1) | copy-start | bytes 6291460
  0.6 0.8 copy-start.3
  2.1 21.0 %all-to-all-start = ((s32[128,1,128]{2,1,0:T(1,128)}), s32[128,1,128]{2,1,0:T(1,128)S(1)}, u32[]{:S(2)}, u32[]{:S(2)}) async-start(s32[128,1,128]{2,1,0:T(1,128)} %spread.1), calls=%async_computation | async-start | bytes 131072 | tf_op jit(solution)/shard_map/all_to_all | solution.py:230
  13.6 1.0 copy-start.1
  14.7 0.7 copy-start.4
  26.5 5.6 %copy-start.6 = (bf16[2048]{0:T(1024)(128)(2,1)S(1)}, bf16[2048]{0:T(1024)(128)(2,1)}, u32[]{:S(2)}) copy-start(bf16[2048]{0:T(1024)(128)(2,1)} %param.10) | copy-start | bytes 12292
  26.6 57.2 %all-to-all-start.1 = ((bf16[128,2,8,1024]{3,2,1,0:T(8,128)(2,1)}), bf16[128,2,8,1024]{3,2,1,0:T(8,128)(2,1)}, u32[]{:S(2)}, u32[]{:S(2)}) async-start(bf16[128,2,8,1024]{3,2,1,0:T(8,128)(2,1)} %rows.1), calls=%async_computation.1 | async-start | bytes 8388608 | tf_op jit(solution)/shard_map/all_to_all | solution.py:230
  32.1 51.6 %copy-start.2 = (bf16[1,128,2048]{2,1,0:T(8,128)(2,1)S(1)}, bf16[1,128,2048]{2,1,0:T(8,128)(2,1)}, u32[]{:S(2)}) copy-start(bf16[1,128,2048]{2,1,0:T(8,128)(2,1)} %param.6) | copy-start | bytes 1572868
  32.1 51.6 %copy-start.5 = (s32[1,128]{1,0:T(1,128)S(1)}, s32[1,128]{1,0:T(1,128)}, u32[]{:S(2)}) copy-start(s32[1,128]{1,0:T(1,128)} %ids_ref.5) | copy-start | bytes 1540
  89.7 6.7 %collective-permute-start = (bf16[128,384]{1,0:T(8,128)(2,1)S(1)}, bf16[128,384]{1,0:T(8,128)(2,1)S(1)}, u32[]{:S(2)}, u32[]{:S(2)}) collective-permute-start(bf16[128,384]{1,0:T(8,128)(2,1)S(1)} %get-tuple-element.17), channel_id=1, source_target_pairs={{0,1},{1,2},{2,3},{3,4},{4,5},{5,6},{6,7},{7,0},{8,9},{9,10},{10,1... | collective-permute-start | bytes 294920 | tf_op jit(solution)/shard_map/ppermute | solution.py:236
  90.5 6.4 %collective-permute-start.1 = (bf16[128,384]{1,0:T(8,128)(2,1)S(1)}, bf16[128,384]{1,0:T(8,128)(2,1)S(1)}, u32[]{:S(2)}, u32[]{:S(2)}) collective-permute-start(bf16[128,384]{1,0:T(8,128)(2,1)S(1)} %get-tuple-element.18), channel_id=1, source_target_pairs={{0,2},{1,3},{2,4},{3,5},{4,6},{5,7},{6,0},{7,1},{8,10},{9,11},{10,... | collective-permute-start | bytes 294920 | tf_op jit(solution)/shard_map/ppermute | solution.py:236
  91.5 6.6 %collective-permute-start.2 = (bf16[128,384]{1,0:T(8,128)(2,1)S(1)}, bf16[128,384]{1,0:T(8,128)(2,1)S(1)}, u32[]{:S(2)}, u32[]{:S(2)}) collective-permute-start(bf16[128,384]{1,0:T(8,128)(2,1)S(1)} %get-tuple-element.19), channel_id=1, source_target_pairs={{0,3},{1,4},{2,5},{3,6},{4,7},{5,0},{6,1},{7,2},{8,11},{9,12},{10,... | collective-permute-start | bytes 294920 | tf_op jit(solution)/shard_map/ppermute | solution.py:236
  93.4 8.4 %collective-permute-start.3 = (bf16[128,384]{1,0:T(8,128)(2,1)S(1)}, bf16[128,384]{1,0:T(8,128)(2,1)S(1)}, u32[]{:S(2)}, u32[]{:S(2)}) collective-permute-start(bf16[128,384]{1,0:T(8,128)(2,1)S(1)} %get-tuple-element.20), channel_id=1, source_target_pairs={{0,4},{1,5},{2,6},{3,7},{4,0},{5,1},{6,2},{7,3},{8,12},{9,13},{10,... | collective-permute-start | bytes 294920 | tf_op jit(solution)/shard_map/ppermute | solution.py:236
  93.8 8.6 %collective-permute-start.4 = (bf16[128,384]{1,0:T(8,128)(2,1)S(1)}, bf16[128,384]{1,0:T(8,128)(2,1)S(1)}, u32[]{:S(2)}, u32[]{:S(2)}) collective-permute-start(bf16[128,384]{1,0:T(8,128)(2,1)S(1)} %get-tuple-element.21), channel_id=1, source_target_pairs={{0,5},{1,6},{2,7},{3,0},{4,1},{5,2},{6,3},{7,4},{8,13},{9,14},{10,... | collective-permute-start | bytes 294920 | tf_op jit(solution)/shard_map/ppermute | solution.py:236
  96.4 6.0 %collective-permute-start.5 = (bf16[128,384]{1,0:T(8,128)(2,1)S(1)}, bf16[128,384]{1,0:T(8,128)(2,1)S(1)}, u32[]{:S(2)}, u32[]{:S(2)}) collective-permute-start(bf16[128,384]{1,0:T(8,128)(2,1)S(1)} %get-tuple-element.22), channel_id=1, source_target_pairs={{0,6},{1,7},{2,0},{3,1},{4,2},{5,3},{6,4},{7,5},{8,14},{9,15},{10,... | collective-permute-start | bytes 294920 | tf_op jit(solution)/shard_map/ppermute | solution.py:236
  96.9 6.3 %collective-permute-start.6 = (bf16[128,384]{1,0:T(8,128)(2,1)S(1)}, bf16[128,384]{1,0:T(8,128)(2,1)S(1)}, u32[]{:S(2)}, u32[]{:S(2)}) collective-permute-start(bf16[128,384]{1,0:T(8,128)(2,1)S(1)} %get-tuple-element.23), channel_id=1, source_target_pairs={{0,7},{1,0},{2,1},{3,2},{4,3},{5,4},{6,5},{7,6},{8,15},{9,8},{10,9... | collective-permute-start | bytes 294920 | tf_op jit(solution)/shard_map/ppermute | solution.py:236
  105.7 10.8 %all-to-all-start.2 = ((bf16[8,128,128]{2,1,0:T(8,128)(2,1)}), bf16[8,128,128]{2,1,0:T(8,128)(2,1)S(1)}, u32[]{:S(2)}, u32[]{:S(2)}) async-start(bf16[8,128,128]{2,1,0:T(8,128)(2,1)} %bitcast.6), calls=%async_computation.2 | async-start | bytes 524288 | tf_op jit(solution)/shard_map/all_to_all | solution.py:230

commit v7 on v6

--- a/solution.py
+++ b/solution.py
@@ -13,7 +13,7 @@
 TILE = 2 * CAP
 HALF = 1024
 MB = 1024 * 1024
-AHEAD = 4
+AHEAD = 3
 BOTH = ("ctx", "table")
 
 
@@ -289,7 +289,7 @@
         2 * MB,
         name="prepare",
     )(all_ids, norm_gain.reshape(1, width))
-    w_blocks = 8
+    w_blocks = 4
     qkv = call(
         functools.partial(qkv_kernel, held),
         [shape((tokens, 3 * HEAD), bf16)] * HEADS,

time: 118 us -> 118 us (level)
  no operation moved by 1% of the time
where the time goes in v7:
time: 118 us; the launch traced here: 117 us
  waiting for transfers between devices  61.4 us (52%)
  starting transfers between devices  29.1 us (25%)
  Pallas kernels  23.7 us (20%)
  local copies, waits for them, and re-layouts  2.52 us (2%)
    all_to_all x3, waiting for transfers between devices, exchange(): return lax.all_to_all(x, axes, split_axis=0, concat_axis=0, tiled=True)  55.8 us
    all_to_all x3, starting transfers between devices, exchange(): return lax.all_to_all(x, axes, split_axis=0, concat_axis=0, tiled=True)  21.3 us
    ppermute x7, starting transfers between devices, shift_all(): lax.ppermute(pieces[k], 'ctx', [(i, (i + k) % n) for i in range(n)])  7.82 us
    pallas_call x1, Pallas kernels, shards(): call(functools.partial(qkv_kernel, held), [shape((tokens, 3 * HEAD), bf16...  6.18 us
    pallas_call x1, Pallas kernels, shards(): call(grad_kernel, shape((held, width), f32), 2 * slots * held * width, 6...  6.17 us
    ppermute x7, waiting for transfers between devices, shift_all(): lax.ppermute(pieces[k], 'ctx', [(i, (i + k) % n) for i in range(n)])  5.62 us
    pallas_call x1, Pallas kernels, shards(): call(rows_kernel, blocks, 2 * slots * held * width, 4 * MB, name='rows',...  3.42 us
    pallas_call x1, Pallas kernels, shards(): call(functools.partial(pack_kernel, held), blocks, 2 * slots * tokens * w...  2.68 us
  transfers between devices with their start and end apart: 10, of which 8 were waited for; matrix products, arithmetic and copies ran while one was open for 0% of the time, Pallas kernels for 9%

profile of v7, /device:TPU:1, one launch (start us, length us, event | category | flops | bytes accessed | tf_op | source)
XLA Modules:
  0.0 117.5 jit_solution(13546469804481012743)
XLA Ops:
  0.7 0.8 copy-done.3
  1.4 0.7 spread.1
  2.1 11.5 %all-to-all-start = ((s32[128,1,128]{2,1,0:T(1,128)}), s32[128,1,128]{2,1,0:T(1,128)S(1)}, u32[]{:S(2)}, u32[]{:S(2)}) async-start(s32[128,1,128]{2,1,0:T(1,128)} %spread.1), calls=%async_computation | async-start | bytes 131072 | tf_op jit(solution)/shard_map/all_to_all | solution.py:230
  13.6 1.0 copy-done.1
  14.7 0.7 copy-done.4
  15.3 2.7 %pack.1.cot_hbm = bf16[128,2,8,1024]{3,2,1,0:T(8,128)(2,1)} custom-call(s32[1,128]{1,0:T(1,128)S(1)} %copy-done.4, bf16[128,2048]{1,0:T(8,128)(2,1)S(1)} %bitcast.4), custom_call_target="tpu_custom_call" | custom-call | flops 536870912 | bytes 3145728 | tf_op jit(solution)/shard_map/pack/pallas_call | solution.py:263
  18.0 5.1 %all-to-all-done.ids_ref = s32[128,1,128]{2,1,0:T(1,128)S(1)} async-done(((s32[128,1,128]{2,1,0:T(1,128)}), s32[128,1,128]{2,1,0:T(1,128)S(1)}, u32[]{:S(2)}, u32[]{:S(2)}) %all-to-all-start) | async-done | bytes 65568 | tf_op jit(solution)/shard_map/all_to_all | solution.py:230
  23.1 3.4 %rows.1 = bf16[128,2,8,1024]{3,2,1,0:T(8,128)(2,1)} custom-call(s32[128,1,128]{2,1,0:T(1,128)S(1)} %all-to-all-done.ids_ref, bf16[512,2048]{1,0:T(8,128)(2,1)S(1)} %copy-done, bf16[128,2,8,1024]{3,2,1,0:T(8,128)(2,1)} %pack.1.cot_hbm), custom_call_target="tpu_custom_call", output_to_operand_aliasing={{}: (2, {})} | custom-call | flops 2147483648 | bytes 4194304 | tf_op jit(solution)/shard_map/rows/pallas_call | solution.py:273
  26.6 5.5 %all-to-all-start.1 = ((bf16[128,2,8,1024]{3,2,1,0:T(8,128)(2,1)}), bf16[128,2,8,1024]{3,2,1,0:T(8,128)(2,1)}, u32[]{:S(2)}, u32[]{:S(2)}) async-start(bf16[128,2,8,1024]{3,2,1,0:T(8,128)(2,1)} %rows.1), calls=%async_computation.1 | async-start | bytes 8388608 | tf_op jit(solution)/shard_map/all_to_all | solution.py:230
  32.2 1.3 %prepare.1 = (bf16[512,1024]{1,0:T(8,128)(2,1)S(1)}, bf16[512,1024]{1,0:T(8,128)(2,1)S(1)}, f32[8,2048]{1,0:T(8,128)S(1)}) custom-call(s32[128,1,128]{2,1,0:T(1,128)S(1)} %all-to-all-done.ids_ref, bf16[1,2048]{1,0:T(2,128)(2,1)S(1)} %reshape.10.gain_ref), custom_call_target="tpu_custom_call" | custom-call | flops 20971520000 | bytes 2097152 | tf_op jit(solution)/shard_map/prepare/pallas_call | solution.py:285
  33.5 50.3 %all-to-all-done.1.got_hbm.cot_ref = bf16[128,2,8,1024]{3,2,1,0:T(8,128)(2,1)} async-done(((bf16[128,2,8,1024]{3,2,1,0:T(8,128)(2,1)}), bf16[128,2,8,1024]{3,2,1,0:T(8,128)(2,1)}, u32[]{:S(2)}, u32[]{:S(2)}) %all-to-all-start.1) | async-done | bytes 4194336 | tf_op jit(solution)/shard_map/all_to_all | solution.py:230
  83.8 6.2 %qkv.1 = (bf16[128,384]{1,0:T(8,128)(2,1)S(1)}, bf16[128,384]{1,0:T(8,128)(2,1)S(1)}, bf16[128,384]{1,0:T(8,128)(2,1)S(1)}, bf16[128,384]{1,0:T(8,128)(2,1)S(1)}...) custom-call(s32[1,128]{1,0:T(1,128)S(1)} %copy-done.5, ...), custom_call_target="tpu_custom_call" | custom-call | flops 1610612736 | bytes 16777216 | tf_op jit(solution)/shard_map/qkv/pallas_call | solution.py:293
  90.0 0.7 collective-permute-start
  90.7 1.1 collective-permute-start.1
  91.8 1.8 %collective-permute-start.2 = (bf16[128,384]{1,0:T(8,128)(2,1)S(1)}, bf16[128,384]{1,0:T(8,128)(2,1)S(1)}, u32[]{:S(2)}, u32[]{:S(2)}) collective-permute-start(bf16[128,384]{1,0:T(8,128)(2,1)S(1)} %get-tuple-element.19), channel_id=1, source_target_pairs={{0,3},{1,4},{2,5},{3,6},{4,7},{5,0},{6,1},{7,2},{8,11},{9,12},{10,... | collective-permute-start | bytes 294920 | tf_op jit(solution)/shard_map/ppermute | solution.py:236
  94.0 2.6 %collective-permute-start.4 = (bf16[128,384]{1,0:T(8,128)(2,1)S(1)}, bf16[128,384]{1,0:T(8,128)(2,1)S(1)}, u32[]{:S(2)}, u32[]{:S(2)}) collective-permute-start(bf16[128,384]{1,0:T(8,128)(2,1)S(1)} %get-tuple-element.21), channel_id=1, source_target_pairs={{0,5},{1,6},{2,7},{3,0},{4,1},{5,2},{6,3},{7,4},{8,13},{9,14},{10,... | collective-permute-start | bytes 294920 | tf_op jit(solution)/shard_map/ppermute | solution.py:236
  97.1 1.1 collective-permute-start.6
  98.4 3.6 %collective-permute-done.3.refs_4_ = bf16[128,384]{1,0:T(8,128)(2,1)S(1)} collective-permute-done((bf16[128,384]{1,0:T(8,128)(2,1)S(1)}, bf16[128,384]{1,0:T(8,128)(2,1)S(1)}, u32[]{:S(2)}, u32[]{:S(2)}) %collective-permute-start.3) | collective-permute-done | bytes 98336 | tf_op jit(solution)/shard_map/ppermute | solution.py:236
  102.0 0.6 collective-permute-done.4.refs_5_
  102.6 0.8 collective-permute-done.6.refs_7_
  103.4 2.5 %attention.1 = bf16[1024,128]{1,0:T(8,128)(2,1)} custom-call(bf16[128,384]{1,0:T(8,128)(2,1)S(1)} %get-tuple-element.16.refs_0_, bf16[128,384]{1,0:T(8,128)(2,1)S(1)} %collective-permute-done.refs_1_, bf16[128,384]{1,0:T(8,128)(2,1)S(1)} %collective-permute-done.1.refs_2_, bf16[128,384]{1,0:T(8,128)(2,1)S(1)} %collective-permute-done.2.refs_3_, ...), custom_call_target="tpu_custom_call" | custom-call | flops 536870912 | bytes 2097152 | tf_op jit(solution)/shard_map/attention/pallas_call | solution.py:334
  105.9 4.3 %all-to-all-start.2 = ((bf16[8,128,128]{2,1,0:T(8,128)(2,1)}), bf16[8,128,128]{2,1,0:T(8,128)(2,1)S(1)}, u32[]{:S(2)}, u32[]{:S(2)}) async-start(bf16[8,128,128]{2,1,0:T(8,128)(2,1)} %bitcast.6), calls=%async_computation.2 | async-start | bytes 524288 | tf_op jit(solution)/shard_map/all_to_all | solution.py:230
  110.2 6.2 %grad.1 = f32[512,2048]{1,0:T(8,128)} custom-call(bf16[512,1024]{1,0:T(8,128)(2,1)S(1)} %get-tuple-element.14.low_hbm.low_ref, bf16[512,1024]{1,0:T(8,128)(2,1)S(1)} %get-tuple-element.15.high_hbm.high_ref, bf16[128,2,8,1024]{3,2,1,0:T(8,128)(2,1)} %all-to-all-done.1.got_hbm.cot_ref), custom_call_target="tpu_custom_call" | custom-call | flops 2147483648 | bytes 6291456 | tf_op jit(solution)/shard_map/grad/pallas_call | solution.py:320
  116.7 0.8 join.1
  (19 shorter events, 1.5 us)
Async XLA Ops:
  0.6 22.5 %copy-start = (bf16[512,2048]{1,0:T(8,128)(2,1)S(1)}, bf16[512,2048]{1,0:T(8,128)(2,1)}, u32[]{:S(2)}) copy-start(bf16[512,2048]{1,0:T(8,128)(2,1)} %table_ref.1) | copy-start | bytes 6291460
  0.6 0.8 copy-start.3
  2.1 21.0 %all-to-all-start = ((s32[128,1,128]{2,1,0:T(1,128)}), s32[128,1,128]{2,1,0:T(1,128)S(1)}, u32[]{:S(2)}, u32[]{:S(2)}) async-start(s32[128,1,128]{2,1,0:T(1,128)} %spread.1), calls=%async_computation | async-start | bytes 131072 | tf_op jit(solution)/shard_map/all_to_all | solution.py:230
  13.6 1.0 copy-start.1
  14.7 0.7 copy-start.4
  26.5 5.6 %copy-start.6 = (bf16[2048]{0:T(1024)(128)(2,1)S(1)}, bf16[2048]{0:T(1024)(128)(2,1)}, u32[]{:S(2)}) copy-start(bf16[2048]{0:T(1024)(128)(2,1)} %param.10) | copy-start | bytes 12292
  26.6 57.2 %all-to-all-start.1 = ((bf16[128,2,8,1024]{3,2,1,0:T(8,128)(2,1)}), bf16[128,2,8,1024]{3,2,1,0:T(8,128)(2,1)}, u32[]{:S(2)}, u32[]{:S(2)}) async-start(bf16[128,2,8,1024]{3,2,1,0:T(8,128)(2,1)} %rows.1), calls=%async_computation.1 | async-start | bytes 8388608 | tf_op jit(solution)/shard_map/all_to_all | solution.py:230
  32.1 51.6 %copy-start.2 = (bf16[1,128,2048]{2,1,0:T(8,128)(2,1)S(1)}, bf16[1,128,2048]{2,1,0:T(8,128)(2,1)}, u32[]{:S(2)}) copy-start(bf16[1,128,2048]{2,1,0:T(8,128)(2,1)} %param.6) | copy-start | bytes 1572868
  32.1 51.6 %copy-start.5 = (s32[1,128]{1,0:T(1,128)S(1)}, s32[1,128]{1,0:T(1,128)}, u32[]{:S(2)}) copy-start(s32[1,128]{1,0:T(1,128)} %ids_ref.5) | copy-start | bytes 1540
  90.0 6.7 %collective-permute-start = (bf16[128,384]{1,0:T(8,128)(2,1)S(1)}, bf16[128,384]{1,0:T(8,128)(2,1)S(1)}, u32[]{:S(2)}, u32[]{:S(2)}) collective-permute-start(bf16[128,384]{1,0:T(8,128)(2,1)S(1)} %get-tuple-element.17), channel_id=1, source_target_pairs={{0,1},{1,2},{2,3},{3,4},{4,5},{5,6},{6,7},{7,0},{8,9},{9,10},{10,1... | collective-permute-start | bytes 294920 | tf_op jit(solution)/shard_map/ppermute | solution.py:236
  90.7 6.4 %collective-permute-start.1 = (bf16[128,384]{1,0:T(8,128)(2,1)S(1)}, bf16[128,384]{1,0:T(8,128)(2,1)S(1)}, u32[]{:S(2)}, u32[]{:S(2)}) collective-permute-start(bf16[128,384]{1,0:T(8,128)(2,1)S(1)} %get-tuple-element.18), channel_id=1, source_target_pairs={{0,2},{1,3},{2,4},{3,5},{4,6},{5,7},{6,0},{7,1},{8,10},{9,11},{10,... | collective-permute-start | bytes 294920 | tf_op jit(solution)/shard_map/ppermute | solution.py:236
  91.8 6.6 %collective-permute-start.2 = (bf16[128,384]{1,0:T(8,128)(2,1)S(1)}, bf16[128,384]{1,0:T(8,128)(2,1)S(1)}, u32[]{:S(2)}, u32[]{:S(2)}) collective-permute-start(bf16[128,384]{1,0:T(8,128)(2,1)S(1)} %get-tuple-element.19), channel_id=1, source_target_pairs={{0,3},{1,4},{2,5},{3,6},{4,7},{5,0},{6,1},{7,2},{8,11},{9,12},{10,... | collective-permute-start | bytes 294920 | tf_op jit(solution)/shard_map/ppermute | solution.py:236
  93.6 8.4 %collective-permute-start.3 = (bf16[128,384]{1,0:T(8,128)(2,1)S(1)}, bf16[128,384]{1,0:T(8,128)(2,1)S(1)}, u32[]{:S(2)}, u32[]{:S(2)}) collective-permute-start(bf16[128,384]{1,0:T(8,128)(2,1)S(1)} %get-tuple-element.20), channel_id=1, source_target_pairs={{0,4},{1,5},{2,6},{3,7},{4,0},{5,1},{6,2},{7,3},{8,12},{9,13},{10,... | collective-permute-start | bytes 294920 | tf_op jit(solution)/shard_map/ppermute | solution.py:236
  94.0 8.6 %collective-permute-start.4 = (bf16[128,384]{1,0:T(8,128)(2,1)S(1)}, bf16[128,384]{1,0:T(8,128)(2,1)S(1)}, u32[]{:S(2)}, u32[]{:S(2)}) collective-permute-start(bf16[128,384]{1,0:T(8,128)(2,1)S(1)} %get-tuple-element.21), channel_id=1, source_target_pairs={{0,5},{1,6},{2,7},{3,0},{4,1},{5,2},{6,3},{7,4},{8,13},{9,14},{10,... | collective-permute-start | bytes 294920 | tf_op jit(solution)/shard_map/ppermute | solution.py:236
  96.6 6.0 %collective-permute-start.5 = (bf16[128,384]{1,0:T(8,128)(2,1)S(1)}, bf16[128,384]{1,0:T(8,128)(2,1)S(1)}, u32[]{:S(2)}, u32[]{:S(2)}) collective-permute-start(bf16[128,384]{1,0:T(8,128)(2,1)S(1)} %get-tuple-element.22), channel_id=1, source_target_pairs={{0,6},{1,7},{2,0},{3,1},{4,2},{5,3},{6,4},{7,5},{8,14},{9,15},{10,... | collective-permute-start | bytes 294920 | tf_op jit(solution)/shard_map/ppermute | solution.py:236
  97.1 6.3 %collective-permute-start.6 = (bf16[128,384]{1,0:T(8,128)(2,1)S(1)}, bf16[128,384]{1,0:T(8,128)(2,1)S(1)}, u32[]{:S(2)}, u32[]{:S(2)}) collective-permute-start(bf16[128,384]{1,0:T(8,128)(2,1)S(1)} %get-tuple-element.23), channel_id=1, source_target_pairs={{0,7},{1,0},{2,1},{3,2},{4,3},{5,4},{6,5},{7,6},{8,15},{9,8},{10,9... | collective-permute-start | bytes 294920 | tf_op jit(solution)/shard_map/ppermute | solution.py:236
  105.9 10.8 %all-to-all-start.2 = ((bf16[8,128,128]{2,1,0:T(8,128)(2,1)}), bf16[8,128,128]{2,1,0:T(8,128)(2,1)S(1)}, u32[]{:S(2)}, u32[]{:S(2)}) async-start(bf16[8,128,128]{2,1,0:T(8,128)(2,1)} %bitcast.6), calls=%async_computation.2 | async-start | bytes 524288 | tf_op jit(solution)/shard_map/all_to_all | solution.py:230
